TPU v7x, 128 devices: a whole 4x4x4 slice. The times are simulated.
128 devices in a mesh: sx: 16 (over z_hi, y, core), sy: 8 (over x, z_lo).
Axes of the slice: x: 4, y: 4, z: 4 (z_hi: 2, z_lo: 2; z = z_hi * 2 + z_lo), core: 2. Of those that a mesh axis runs over, the one named last changes fastest.
Arguments:
- vectors: bfloat16 [64, 128, 256, 128], P(None, 'sx', 'sy'), may hold values from -0.4453125 to 0.4453125
- root_stiff: float32 [128, 256, 128], P('sx', 'sy'), may hold values from 0.5 to 2
- diag_coef: float32 [128, 256, 128], P('sx', 'sy'), may hold values from -3 to 3
- counts: int32 [16, 8], P('sx', 'sy'), may hold values from 8 to 64, as said below
Outputs:
- own_block: float32 [16, 8, 64, 64], P('sx', 'sy')
- face_blocks: float32 [16, 8, 64, 256], P('sx', 'sy')
- corner_blocks: float32 [16, 8, 64, 256], P('sx', 'sy')
- offsets: int32 [16, 8], P('sx', 'sy')
Inputs may be any that keep to these rules, and one draw needn't show every extreme that they name: Some subdomain has exactly 64 eigenvectors in every draw; small counts are more common than large ones.
All inputs are finite; a program needn't handle non-finite values.
Results may differ from a plain program's by a relative error of at most 0.007.
Values may be sent and summed in bfloat16 or wider, within the bound.
A program may use at most 128 MiB of HBM per device.

v0:
```python
import jax
import jax.numpy as jnp
from jax import lax
from jax.sharding import PartitionSpec as P


def extended(cells, sides, width):
    for axis, dim in sides:
        count = lax.axis_size(axis)
        ends = count - 1
        head = lax.slice_in_dim(cells, 0, width, axis=dim)
        tail = lax.slice_in_dim(cells, cells.shape[dim] - width, cells.shape[dim], axis=dim)
        cells = jnp.concatenate(
            [
                lax.ppermute(tail, axis, [(i, (i + 1) % count) for i in range(ends)]),
                cells,
                lax.ppermute(head, axis, [((i + 1) % count, i) for i in range(ends)]),
            ],
            axis=dim,
        )
    return cells


def entering(value, axis, join, neutral):
    count, mine = (lax.axis_size(axis), lax.axis_index(axis))
    pieces = lax.all_gather(value, axis)
    total = jnp.full_like(value, 0) + jnp.asarray(neutral, value.dtype)

    def step(position, total):
        longer = join(total, pieces[position])
        return jnp.where(position < mine, longer, total)

    return lax.fori_loop(0, count - 1, step, total)


def smooth_along(values, dim_index):
    length = values.shape[dim_index]
    zero_slab = jnp.zeros_like(lax.slice_in_dim(values, 0, 1, axis=dim_index))
    below_side = jnp.concatenate(
        [zero_slab, lax.slice_in_dim(values, 0, length - 1, axis=dim_index)], axis=dim_index
    )
    above_side = jnp.concatenate(
        [lax.slice_in_dim(values, 1, length, axis=dim_index), zero_slab], axis=dim_index
    )
    return values + 0.5 * (below_side + above_side)


def own_term(masked, scaled, stiff_here, diag_here):
    scaled_wide = scaled.astype(jnp.float32)
    smoothed = smooth_along(smooth_along(smooth_along(scaled_wide, 1), 2), 3)
    beside = smoothed - scaled_wide
    applied = (diag_here[None] * masked.astype(jnp.float32) - stiff_here[None] * beside).astype(
        jnp.bfloat16
    )
    vec_rows = masked.shape[0]
    return lax.dot_general(
        masked.reshape(vec_rows, -1),
        applied.reshape(vec_rows, -1),
        (((1,), (1,)), ((), ())),
        preferred_element_type=jnp.float32,
    )


def face_term(own_layer, near_layer):
    weighted = 0.5 * smooth_along(smooth_along(near_layer.astype(jnp.float32), 1), 2)
    vec_rows = own_layer.shape[0]
    return -lax.dot_general(
        own_layer.astype(jnp.float32).reshape(vec_rows, -1),
        weighted.reshape(vec_rows, -1),
        (((1,), (1,)), ((), ())),
        precision=lax.Precision.HIGHEST,
        preferred_element_type=jnp.float32,
    )


def corner_term(own_column, near_column):
    weighted = 0.25 * smooth_along(near_column.astype(jnp.float32), 1)
    return -lax.dot_general(
        own_column.astype(jnp.float32),
        weighted,
        (((1,), (1,)), ((), ())),
        precision=lax.Precision.HIGHEST,
        preferred_element_type=jnp.float32,
    )


def on_device(vectors, root_stiff, diag_coef, counts):
    vec_rows = vectors.shape[0]
    live_count = counts[0, 0]
    row_index = lax.broadcasted_iota(jnp.int32, (vec_rows, 1, 1, 1), 0)
    masked = jnp.where(row_index < live_count, vectors, jnp.zeros_like(vectors))
    scaled = (root_stiff[None] * masked.astype(jnp.float32)).astype(jnp.bfloat16)
    padded = extended(scaled, (("sx", 1), ("sy", 2)), 1)
    own_block = own_term(masked, scaled, root_stiff, diag_coef)
    faces = [
        face_term(scaled[:, 0], padded[:, 0, 1:-1]),
        face_term(scaled[:, -1], padded[:, -1, 1:-1]),
        face_term(scaled[:, :, 0], padded[:, 1:-1, 0]),
        face_term(scaled[:, :, -1], padded[:, 1:-1, -1]),
    ]
    corners = [
        corner_term(scaled[:, 0, 0], padded[:, 0, 0]),
        corner_term(scaled[:, 0, -1], padded[:, 0, -1]),
        corner_term(scaled[:, -1, 0], padded[:, -1, 0]),
        corner_term(scaled[:, -1, -1], padded[:, -1, -1]),
    ]
    offsets = entering(
        counts, "sy", lambda earlier, later: earlier + later, jnp.zeros((1, 1), jnp.int32)
    )
    return (
        own_block[None, None],
        jnp.concatenate(faces, axis=1)[None, None],
        jnp.concatenate(corners, axis=1)[None, None],
        offsets,
    )


def solution(mesh):
    return jax.shard_map(
        on_device,
        mesh=mesh,
        in_specs=(
            P(None, "sx", "sy", None),
            P("sx", "sy", None),
            P("sx", "sy", None),
            P("sx", "sy"),
        ),
        out_specs=(
            P("sx", "sy", None, None),
            P("sx", "sy", None, None),
            P("sx", "sy", None, None),
            P("sx", "sy"),
        ),
        check_vma=False,
    )
```

profile of v0, /device:TPU:64, one launch (start us, length us, event | category | flops | bytes accessed | tf_op | source)
XLA Modules:
  0.0 127.3 jit_solution(864712971653260280)
XLA Ops:
  1.3 8.9 %fusion.2 = (bf16[64,8,32,128]{3,0,2,1:T(8,128)(2,1)S(1)}, f32[64,8,32,128]{3,0,2,1:T(8,128)}) fusion(f32[8,32,128]{2,1,0:T(8,128)} %param.7, bf16[64,8,32,128]{3,2,1,0:T(8,128)(2,1)} %param.6, pred[64]{0:T(512)(128)(4,1)S(1)} %iota_compare_fusion), kind=kLoop, calls=%fused_computation.5 | loop fusion | flops 10485760 | bytes 16908352 | tf_op jit(solution)/shard_map/convert_element_type | solution.py:92
  10.2 0.0 copy-start.1
  10.2 2.0 %copy-done.1 = bf16[64,8,32,128]{3,0,2,1:T(8,128)(2,1)} copy-done((bf16[64,8,32,128]{3,0,2,1:T(8,128)(2,1)}, bf16[64,8,32,128]{3,0,2,1:T(8,128)(2,1)S(1)}, u32[]{:S(2)}) %copy-start.1) | copy-done | bytes 4194328
  12.2 0.1 fusion.91
  12.3 1.9 %collective-permute-start = (bf16[64,1,32,128]{3,0,2,1:T(8,128)(2,1)S(1)}, bf16[64,1,32,128]{3,0,2,1:T(8,128)(2,1)S(1)}, u32[]{:S(2)}, u32[]{:S(2)}) collective-permute-start(bf16[64,1,32,128]{3,0,2,1:T(8,128)(2,1)S(1)} %get-tuple-element.116), channel_id=1, source_target_pairs={{0,8},{8,16},{16,24},{24,32},{32,40},{40,48},{48,56},{56,64},{64,7... | collective-permute-start | bytes 1572872 | tf_op jit(solution)/shard_map/ppermute | solution.py:15
  14.2 7.3 %collective-permute-start.1 = (bf16[64,1,32,128]{3,0,2,1:T(8,128)(2,1)S(1)}, bf16[64,1,32,128]{3,0,2,1:T(8,128)(2,1)S(1)}, u32[]{:S(2)}, u32[]{:S(2)}) collective-permute-start(bf16[64,1,32,128]{3,0,2,1:T(8,128)(2,1)S(1)} %get-tuple-element.117), channel_id=1, source_target_pairs={{8,0},{16,8},{24,16},{32,24},{40,32},{48,40},{56,48},{64,56},{72,6... | collective-permute-start | bytes 1572872 | tf_op jit(solution)/shard_map/ppermute | solution.py:17
  21.5 0.0 copy-start.2
  21.5 13.6 %fusion.89 = (f32[64,7,32,128]{3,0,2,1:T(8,128)}, f32[64,7,32,128]{3,0,2,1:T(8,128)}) fusion(f32[64,8,32,128]{3,0,2,1:T(8,128)} %get-tuple-element.113), kind=kLoop, calls=%fused_computation.122 | loop fusion | bytes 29360128 | tf_op jit(solution)/shard_map/slice | solution.py:40
  35.1 0.0 copy-done.2
  35.1 8.5 %multiply_add_fusion.1 = f32[64,8,32,128]{3,0,2,1:T(8,128)S(1)} fusion(f32[64,7,32,128]{3,0,2,1:T(8,128)} %get-tuple-element.109, f32[64,7,32,128]{3,0,2,1:T(8,128)} %get-tuple-element.108, bf16[64,8,32,128]{3,2,1,0:T(8,128)(2,1)} %param.6, pred[64]{0:T(512)(128)(4,1)S(1)} %iota_compare_fusion, f32[8,32,128]{2,1,0:T(8,128)S(1)} %copy-done.2), kind=kLoop, calls=%fused_computation.7 | loop fusion | flops 16777216 | bytes 27394112 | tf_op jit(solution)/shard_map/add | solution.py:45
  43.6 6.6 %fusion.88 = (f32[64,8,31,128]{3,0,2,1:T(8,128)}, f32[64,8,31,128]{3,0,2,1:T(8,128)}) fusion(f32[64,8,32,128]{3,0,2,1:T(8,128)S(1)} %multiply_add_fusion.1), kind=kLoop, calls=%fused_computation.121 | loop fusion | bytes 32505856 | tf_op jit(solution)/shard_map/slice | solution.py:40
  50.2 7.2 %multiply_add_fusion = f32[64,8,32,128]{3,0,2,1:T(8,128)S(1)} fusion(f32[64,8,32,128]{3,0,2,1:T(8,128)S(1)} %multiply_add_fusion.1, f32[64,8,31,128]{3,0,2,1:T(8,128)} %get-tuple-element.107, f32[64,8,31,128]{3,0,2,1:T(8,128)} %get-tuple-element.106), kind=kLoop, calls=%fused_computation.6 | loop fusion | flops 6291456 | bytes 33030144 | tf_op jit(solution)/shard_map/add | solution.py:45
  57.5 0.0 copy-start
  57.5 3.3 %copy-done = f32[64,8,32,128]{3,0,2,1:T(8,128)} copy-done((f32[64,8,32,128]{3,0,2,1:T(8,128)}, f32[64,8,32,128]{3,0,2,1:T(8,128)S(1)}, u32[]{:S(2)}) %copy-start) | copy-done | bytes 8388632
  60.7 0.0 copy-start.4
  60.7 7.3 %fusion.87 = (f32[64,8,32,127]{3,0,2,1:T(8,128)}, f32[64,8,32,127]{3,0,2,1:T(8,128)}) fusion(f32[64,8,32,128]{3,0,2,1:T(8,128)S(1)} %multiply_add_fusion), kind=kLoop, calls=%fused_computation.120 | loop fusion | bytes 33292288 | tf_op jit(solution)/shard_map/slice | solution.py:40
  68.0 0.0 copy-done.4
  68.0 0.6 dynamic-slice
  68.6 0.9 bitcast_dynamic-update-slice_fusion
  69.5 0.0 copy-done.3
  69.5 15.0 %fusion.9 = f32[1,1,64,64]{3,2,1,0:T(8,128)} fusion(f32[64,8,32,128]{3,0,2,1:T(8,128)} %copy-done, f32[64,8,32,127]{3,0,2,1:T(8,128)} %get-tuple-element.105, f32[64,8,32,127]{3,0,2,1:T(8,128)} %get-tuple-element.104, f32[8,32,128]{2,1,0:T(8,128)S(1)} %copy-done.2, f32[8,32,128]{2,1,0:T(8,128)S(1)} %copy-done.3, bf16[64,8,32,128]{3,2,1,0:T(8,128)(2,1)} %param.6, ...), kind=kOutput, calls=%fused_computation.16 | convolution fusion | flops 297795584 | bytes 29507648 | tf_op jit(solution)/shard_map/dot_general | solution.py:56
  84.5 11.7 %all-reduce.30 = s32[8]{0:T(128)S(1)} all-reduce(s32[8]{0:T(128)S(1)} %bitcast_dynamic-update-slice_fusion), channel_id=2, replica_groups=mesh['sx'=16,'sy'=8] {'sy'}, use_global_device_ids=true, to_apply=%add.30 | all-reduce | flops 8 | bytes 64
  96.2 0.3 copy.26
  96.5 0.3 copy.24
  96.9 1.0 fusion.90
  97.9 0.1 copy.28
  98.0 0.1 copy.30
  98.1 9.5 %while.13 = (s32[]{:T(128)}, s32[1,1]{1,0:T(1,128)}, s32[]{:T(128)}, s32[8,1,1]{0,2,1:T(1,128)S(1)}, s32[]{:T(128)}) while((s32[]{:T(128)}, s32[1,1]{1,0:T(1,128)}, s32[]{:T(128)}, s32[8,1,1]{0,2,1:T(1,128)S(1)}, s32[]{:T(128)}) %tuple.63), condition=%wide.region_1.2_spmd, body=%wide.region_0.1_spmd.sunk | while | flops 5 | bytes 115 | solution.py:33
  98.1 0.6 constant_dynamic-slice_fusion.2
  99.5 0.6 constant_dynamic-slice_fusion.2
  100.8 0.6 constant_dynamic-slice_fusion.2
  102.2 0.6 constant_dynamic-slice_fusion.2
  103.5 0.6 constant_dynamic-slice_fusion.2
  104.9 0.6 constant_dynamic-slice_fusion.2
  106.2 0.6 constant_dynamic-slice_fusion.2
  107.6 0.0 collective-permute-done
  107.6 0.0 collective-permute-done.1
  107.6 1.0 pad_maximum_fusion.2
  108.6 3.5 %collective-permute-start.2 = (bf16[64,10,1,128]{3,0,2,1:T(8,128)(2,1)S(1)}, bf16[64,10,1,128]{3,0,2,1:T(8,128)(2,1)S(1)}, u32[]{:S(2)}, u32[]{:S(2)}) collective-permute-start(bf16[64,10,1,128]{3,0,2,1:T(8,128)(2,1)S(1)} %get-tuple-element.110), channel_id=1, source_target_pairs={{0,1},{1,2},{2,3},{3,4},{4,5},{5,6},{6,7},{8,9},{9,10},{10,11},{11... | collective-permute-start | bytes 491528 | tf_op jit(solution)/shard_map/ppermute | solution.py:15
  112.2 1.3 %collective-permute-start.3 = (bf16[64,10,1,128]{3,0,2,1:T(8,128)(2,1)S(1)}, bf16[64,10,1,128]{3,0,2,1:T(8,128)(2,1)S(1)}, u32[]{:S(2)}, u32[]{:S(2)}) collective-permute-start(bf16[64,10,1,128]{3,0,2,1:T(8,128)(2,1)S(1)} %get-tuple-element.111), channel_id=1, source_target_pairs={{1,0},{2,1},{3,2},{4,3},{5,4},{6,5},{7,6},{9,8},{10,9},{11,10},{12... | collective-permute-start | bytes 491528 | tf_op jit(solution)/shard_map/ppermute | solution.py:17
  113.5 0.1 bitcast_convert_fusion
  113.6 0.2 fusion.95
  113.9 0.1 bitcast_convert_fusion.1
  114.0 0.2 fusion.93
  114.2 0.3 multiply_add_fusion.3
  114.5 0.4 fusion.92
  114.9 0.3 multiply_add_fusion.2
  115.2 0.4 fusion.94
  115.6 1.0 convolution_negate_fusion.1
  116.7 1.0 convolution_negate_fusion
  117.7 1.7 %collective-permute-done.3 = bf16[64,10,1,128]{3,0,2,1:T(8,128)(2,1)S(1)} collective-permute-done((bf16[64,10,1,128]{3,0,2,1:T(8,128)(2,1)S(1)}, bf16[64,10,1,128]{3,0,2,1:T(8,128)(2,1)S(1)}, u32[]{:S(2)}, u32[]{:S(2)}) %collective-permute-start.3) | collective-permute-done | bytes 163872 | tf_op jit(solution)/shard_map/ppermute | solution.py:17
  119.5 0.0 collective-permute-done.2
  119.6 0.1 fusion.96
  119.8 0.1 fusion.98
  119.9 0.1 fusion.100
  120.0 0.1 fusion.101
  120.1 0.4 convolution_negate_fusion.7
  120.5 0.4 convolution_negate_fusion.6
  120.9 1.0 convolution_negate_fusion.5
  121.9 1.0 convolution_negate_fusion.3
  122.8 1.0 convolution_negate_fusion.4
  123.8 1.0 convolution_negate_fusion.2
  124.8 0.7 maximum_bitcast_fusion.1
  125.5 0.7 maximum_bitcast_fusion
  (11 shorter events, 0.2 us)
Async XLA Ops:
  10.2 2.0 %copy-start.1 = (bf16[64,8,32,128]{3,0,2,1:T(8,128)(2,1)}, bf16[64,8,32,128]{3,0,2,1:T(8,128)(2,1)S(1)}, u32[]{:S(2)}) copy-start(bf16[64,8,32,128]{3,0,2,1:T(8,128)(2,1)S(1)} %get-tuple-element.112) | copy-start | bytes 12582916
  12.3 95.3 %collective-permute-start = (bf16[64,1,32,128]{3,0,2,1:T(8,128)(2,1)S(1)}, bf16[64,1,32,128]{3,0,2,1:T(8,128)(2,1)S(1)}, u32[]{:S(2)}, u32[]{:S(2)}) collective-permute-start(bf16[64,1,32,128]{3,0,2,1:T(8,128)(2,1)S(1)} %get-tuple-element.116), channel_id=1, source_target_pairs={{0,8},{8,16},{16,24},{24,32},{32,40},{40,48},{48,56},{56,64},{64,7... | collective-permute-start | bytes 1572872 | tf_op jit(solution)/shard_map/ppermute | solution.py:15
  14.2 93.4 %collective-permute-start.1 = (bf16[64,1,32,128]{3,0,2,1:T(8,128)(2,1)S(1)}, bf16[64,1,32,128]{3,0,2,1:T(8,128)(2,1)S(1)}, u32[]{:S(2)}, u32[]{:S(2)}) collective-permute-start(bf16[64,1,32,128]{3,0,2,1:T(8,128)(2,1)S(1)} %get-tuple-element.117), channel_id=1, source_target_pairs={{8,0},{16,8},{24,16},{32,24},{40,32},{48,40},{56,48},{64,56},{72,6... | collective-permute-start | bytes 1572872 | tf_op jit(solution)/shard_map/ppermute | solution.py:17
  21.5 13.7 %copy-start.2 = (f32[8,32,128]{2,1,0:T(8,128)S(1)}, f32[8,32,128]{2,1,0:T(8,128)}, u32[]{:S(2)}) copy-start(f32[8,32,128]{2,1,0:T(8,128)} %param.7) | copy-start | bytes 393220
  57.5 3.3 %copy-start = (f32[64,8,32,128]{3,0,2,1:T(8,128)}, f32[64,8,32,128]{3,0,2,1:T(8,128)S(1)}, u32[]{:S(2)}) copy-start(f32[64,8,32,128]{3,0,2,1:T(8,128)S(1)} %multiply_add_fusion) | copy-start | bytes 25165828
  60.7 7.3 %copy-start.4 = (u32[128]{0:T(128)S(1)}, u32[128]{0:T(128)}, u32[]{:S(2)}) copy-start(u32[128]{0:T(128)} %constant.113) | copy-start | bytes 1540
  60.7 8.8 %copy-start.3 = (f32[8,32,128]{2,1,0:T(8,128)S(1)}, f32[8,32,128]{2,1,0:T(8,128)}, u32[]{:S(2)}) copy-start(f32[8,32,128]{2,1,0:T(8,128)} %param.8) | copy-start | bytes 393220
  108.6 10.8 %collective-permute-start.2 = (bf16[64,10,1,128]{3,0,2,1:T(8,128)(2,1)S(1)}, bf16[64,10,1,128]{3,0,2,1:T(8,128)(2,1)S(1)}, u32[]{:S(2)}, u32[]{:S(2)}) collective-permute-start(bf16[64,10,1,128]{3,0,2,1:T(8,128)(2,1)S(1)} %get-tuple-element.110), channel_id=1, source_target_pairs={{0,1},{1,2},{2,3},{3,4},{4,5},{5,6},{6,7},{8,9},{9,10},{10,11},{11... | collective-permute-start | bytes 491528 | tf_op jit(solution)/shard_map/ppermute | solution.py:15
  112.2 7.2 %collective-permute-start.3 = (bf16[64,10,1,128]{3,0,2,1:T(8,128)(2,1)S(1)}, bf16[64,10,1,128]{3,0,2,1:T(8,128)(2,1)S(1)}, u32[]{:S(2)}, u32[]{:S(2)}) collective-permute-start(bf16[64,10,1,128]{3,0,2,1:T(8,128)(2,1)S(1)} %get-tuple-element.111), channel_id=1, source_target_pairs={{1,0},{2,1},{3,2},{4,3},{5,4},{6,5},{7,6},{9,8},{10,9},{11,10},{12... | collective-permute-start | bytes 491528 | tf_op jit(solution)/shard_map/ppermute | solution.py:17
where the time goes:
time: 128 us; the launch traced here: 127 us
  local copies, waits for them, and re-layouts  42.5 us (33%)
  other arithmetic  28.1 us (22%)
  matrix products  21.7 us (17%)
  starting transfers between devices  14 us (11%)
  blocking collectives  11.7 us (9%)
  loops' own time  4.95 us (4%)
  between operations  2.77 us (2%)
  waiting for transfers between devices  1.67 us (1%)
    slice x13, local copies, waits for them, and re-layouts, smooth_along(): lax.slice_in_dim(values, 0, length - 1, axis=dim_index)  29.3 us
    add x6, other arithmetic, smooth_along(): return values + 0.5 * (below_side + above_side)  16.4 us
    dot_general x1, matrix products, own_term(): lax.dot_general(masked.reshape(vec_rows, -1), applied.reshape(vec_rows, -...  15 us
    unnamed x1, blocking collectives  11.7 us
    convert_element_type x1, other arithmetic, on_device(): (root_stiff[None] * masked.astype(jnp.float32)).astype(jnp.bfloat16)  8.93 us
    ppermute x2, starting transfers between devices, extended(): lax.ppermute(head, axis, [((i + 1) % count, i) for i in range(ends)])  8.55 us
    unnamed x13, local copies, waits for them, and re-layouts  6.7 us
    ppermute x2, starting transfers between devices, extended(): lax.ppermute(tail, axis, [(i, (i + 1) % count) for i in range(ends)])  5.46 us
  transfers between devices with their start and end apart: 4, of which 1 were waited for; matrix products, arithmetic and copies ran while one was open for 55% of the time, Pallas kernels for 0%

commit v1 on v0

v1 whole, which is shorter than its diff:
```python
import functools

import jax
import jax.numpy as jnp
from jax import lax
from jax.experimental import pallas as pl
from jax.experimental.pallas import tpu as pltpu
from jax.sharding import PartitionSpec as P

MESH = pl.DeviceIdType.MESH
F32 = jnp.float32
BF16 = jnp.bfloat16
CHUNK = 4


def row_dot(left, right):
    return lax.dot_general(left, right, (((1,), (1,)), ((), ())), preferred_element_type=F32)


def along_lanes(pieces):
    return jnp.concatenate(pieces, axis=1)


def block_dot(left_ref, left_start, right_ref, right_start, count):
    return row_dot(
        along_lanes([left_ref[left_start + i] for i in range(count)]),
        along_lanes([right_ref[right_start + i] for i in range(count)]),
    )


def kernel(
    n_x,
    n_y,
    vec_ref,
    rs_ref,
    dg_ref,
    cnt_ref,
    own_ref,
    face_ref,
    corner_ref,
    off_ref,
    vv,
    rs,
    dg,
    wide,
    mb,
    sb,
    zp,
    ab,
    vx,
    vy,
    sy0,
    rxm,
    rxp,
    rym,
    ryp,
    rc,
    pout,
    pin,
    cb,
    cr,
    load_sem,
    send_sem,
    recv_sem,
    csend_sem,
    crecv_sem,
):
    rows, c_x, c_y, c_z = vec_ref.shape
    half_x, half_y = c_x // 2, c_y // 2
    ix, iy = lax.axis_index("sx"), lax.axis_index("sy")

    order = [0, c_x - 1] + list(range(1, c_x - 1))
    loads = {x: pltpu.make_async_copy(vec_ref.at[:, x], vv.at[x], load_sem.at[x]) for x in order}
    rs_load = pltpu.make_async_copy(rs_ref, rs, load_sem.at[c_x])
    dg_load = pltpu.make_async_copy(dg_ref, dg, load_sem.at[c_x + 1])
    loads[0].start()
    rs_load.start()
    loads[c_x - 1].start()
    for x in order[2:]:
        loads[x].start()
    dg_load.start()

    low_x, high_x = ix > 0, ix < n_x - 1
    low_y, high_y = iy > 0, iy < n_y - 1
    faces = [
        (low_x, (ix - 1, iy)),
        (high_x, (ix + 1, iy)),
        (low_y, (ix, iy - 1)),
        (high_y, (ix, iy + 1)),
    ]
    diagonals = [
        (low_x & low_y, (ix - 1, iy - 1)),
        (low_x & high_y, (ix - 1, iy + 1)),
        (high_x & low_y, (ix + 1, iy - 1)),
        (high_x & high_y, (ix + 1, iy + 1)),
    ]

    barrier = pltpu.get_barrier_semaphore()
    for there, device in faces + diagonals:

        @pl.when(there)
        def _(device=device):
            pl.semaphore_signal(barrier, inc=1, device_id=device, device_id_type=MESH)

    for far in range(2, n_y):

        @pl.when(iy >= far)
        def _(far=far):
            pl.semaphore_signal(barrier, inc=1, device_id=(ix, iy - far), device_id_type=MESH)

    beside = sum(there.astype(jnp.int32) for there, _ in faces + diagonals)
    later = jnp.maximum(n_y - 2 - iy, 0)

    count = cnt_ref[0, 0]
    cb[...] = jnp.full(cb.shape, count, jnp.int32)
    keep = lax.broadcasted_iota(jnp.int32, (rows, c_z), 0) < count
    lane_r = lax.broadcasted_iota(jnp.int32, (c_z, c_z), 0)
    lane_c = lax.broadcasted_iota(jnp.int32, (c_z, c_z), 1)
    apart = jnp.abs(lane_r - lane_c)
    smooth = jnp.where(apart == 0, 1.0, jnp.where(apart == 1, 0.5, 0.0)).astype(BF16)

    def zero_slab(x):
        def step(y, _):
            zp[x, y] = jnp.zeros((rows, c_z), F32)
            return _

        lax.fori_loop(0, c_y + 2, step, 0)

    zero_slab(0)
    zero_slab(c_x + 1)
    for x in range(1, c_x + 1):
        zp[x, 0] = jnp.zeros((rows, c_z), F32)
        zp[x, c_y + 1] = jnp.zeros((rows, c_z), F32)

    def widen(x):
        wide[...] = vv[x].reshape(rows * c_y, c_z).astype(F32)

    def scale(x):
        def step(i, _):
            pieces = []
            for j in range(CHUNK):
                y = i * CHUNK + j
                m = wide[pl.ds(y, rows, stride=c_y), :]
                m = jnp.where(keep, m, 0.0)
                s = (m * rs[x, pl.ds(y, 1), :]).astype(BF16)
                mb[x, y] = m.astype(BF16)
                sb[x, y] = s
                pieces.append(s)
            z = jnp.dot(jnp.concatenate(pieces, axis=0), smooth, preferred_element_type=F32)
            for j in range(CHUNK):
                zp[x + 1, i * CHUNK + j + 1] = z[j * rows : (j + 1) * rows]
            return _

        lax.fori_loop(0, c_y // CHUNK, step, 0)

    rs_load.wait()
    for x in (0, c_x - 1):
        loads[x].wait()
        widen(x)
        scale(x)

    def face_step(y, _):
        vx[y] = (-0.25 * ((zp[c_x, y] + zp[c_x, y + 2]) + 2.0 * zp[c_x, y + 1])).astype(BF16)
        return _

    lax.fori_loop(0, c_y, face_step, 0)

    pl.semaphore_wait(barrier, beside + later)

    def to_face(d, phase, to=None):
        opposite = d ^ 1
        if phase == 0:
            src, dst = [
                (sb.at[0, pl.ds(0, half_y)], rxp),
                (vx.at[pl.ds(half_y, half_y)], rxm),
                (sy0.at[pl.ds(0, half_x)], ryp),
                (vy.at[pl.ds(half_x, half_x)], rym),
            ][d]
        else:
            src, dst = pout.at[d], pin.at[opposite]
        return pltpu.make_async_remote_copy(
            src_ref=src,
            dst_ref=dst,
            send_sem=send_sem.at[phase * 4 + d],
            recv_sem=recv_sem.at[phase * 4 + opposite],
            device_id=faces[d if to is None else to][1],
            device_id_type=MESH,
        )

    def from_face(d, phase):
        return to_face(d ^ 1, phase, d)

    def from_corner(d):
        return to_corner(3 - d, d)

    def to_corner(d, to=None):
        opposite = 3 - d
        x, y = (0, c_x - 1)[d // 2], (0, c_y - 1)[d % 2]
        return pltpu.make_async_remote_copy(
            src_ref=sb.at[x, y],
            dst_ref=rc.at[opposite],
            send_sem=send_sem.at[8 + d],
            recv_sem=recv_sem.at[8 + opposite],
            device_id=diagonals[d if to is None else to][1],
            device_id_type=MESH,
        )

    def to_peer(far):
        return pltpu.make_async_remote_copy(
            src_ref=cb,
            dst_ref=cr.at[far],
            send_sem=csend_sem.at[far],
            recv_sem=crecv_sem.at[far],
            device_id=(ix, iy + far),
            device_id_type=MESH,
        )

    def guarded(there, action):
        @pl.when(there)
        def _():
            action()

    for d in (1, 0):
        guarded(faces[d][0], lambda d=d: to_face(d, 0).start())
    for d in range(4):
        guarded(diagonals[d][0], lambda d=d: to_corner(d).start())
    for far in range(1, n_y):
        guarded(iy + far < n_y, lambda far=far: to_peer(far).start())

    for x in order[2:]:
        loads[x].wait()
        widen(x)
        scale(x)

    for x in range(c_x):
        vy[x] = (
            -0.25 * ((zp[x, c_y] + zp[x + 2, c_y]) + 2.0 * zp[x + 1, c_y])
        ).astype(BF16)
        sy0[x] = sb[x, 0]
    for d in (3, 2):
        guarded(faces[d][0], lambda d=d: to_face(d, 0).start())

    dg_load.wait()
    dg[...] = dg[...] + rs[...] * rs[...]
    rs[...] = rs[...] * 0.25

    def apply_slab(x, total):
        def across(y):
            near = zp[x + 1, y]
            return (zp[x, y] + near) + (near + zp[x + 2, y])

        def step(i, carry):
            g_here, u_before, total = carry
            for j in range(CHUNK):
                y = i * CHUNK + j
                g_next = across(y + 2)
                u_after = g_here + g_next
                q = u_before + u_after
                m = mb[x, y].astype(F32)
                applied = dg[x, pl.ds(y, 1), :] * m - rs[x, pl.ds(y, 1), :] * q
                ab[y] = applied.astype(BF16)
                g_here, u_before = g_next, u_after
            left = along_lanes([mb[x, i * CHUNK + j] for j in range(CHUNK)])
            right = along_lanes([ab[i * CHUNK + j] for j in range(CHUNK)])
            return g_here, u_before, total + row_dot(left, right)

        first = across(1)
        carry = lax.fori_loop(0, c_y // CHUNK, step, (first, first, total))
        return carry[2]

    own_ref[0, 0] = lax.fori_loop(0, c_x, apply_slab, jnp.zeros((rows, rows), F32))

    def half_sum(d):
        from_face(d, 0).wait_recv()
        mine, mine_at, other, depth = [
            (sb.at[0], half_y, rxm, half_y),
            (vx, 0, rxp, half_y),
            (sy0, half_x, rym, half_x),
            (vy, 0, ryp, half_x),
        ][d]
        face_ref[0, 0, :, d * rows : (d + 1) * rows] = block_dot(mine, mine_at, other, 0, depth)
        pout[d, :, 0:rows] = block_dot(other, 0, mine, mine_at, depth)
        to_face(d, 1).start()

    for d in (2, 3, 0, 1):
        guarded(faces[d][0], lambda d=d: half_sum(d))

    for d in range(4):

        def corner_sum(d=d):
            from_corner(d).wait_recv()
            x, y = (0, c_x - 1)[d // 2], (0, c_y - 1)[d % 2]
            mine = (-0.25 * zp[x + 1, y + 1]).astype(BF16)
            corner_ref[0, 0, :, d * rows : (d + 1) * rows] = row_dot(mine, rc[d])

        def corner_zero(d=d):
            corner_ref[0, 0, :, d * rows : (d + 1) * rows] = jnp.zeros((rows, rows), F32)

        guarded(diagonals[d][0], corner_sum)
        guarded(jnp.logical_not(diagonals[d][0]), corner_zero)

    off_ref[...] = jnp.zeros(off_ref.shape, jnp.int32)
    for far in range(1, n_y):

        def earlier(far=far):
            to_peer(far).wait_recv()
            off_ref[...] += cr[far, 0:1, 0:1]

        guarded(iy >= far, earlier)

    def finish(d):
        from_face(d, 1).wait_recv()
        face_ref[0, 0, :, d * rows : (d + 1) * rows] += pin[d, :, 0:rows]

    def face_zero(d):
        face_ref[0, 0, :, d * rows : (d + 1) * rows] = jnp.zeros((rows, rows), F32)

    for d in (2, 3, 0, 1):
        guarded(faces[d][0], lambda d=d: finish(d))
        guarded(jnp.logical_not(faces[d][0]), lambda d=d: face_zero(d))

    def sent(d):
        to_face(d, 0).wait_send()
        to_face(d, 1).wait_send()

    for d in range(4):
        guarded(faces[d][0], lambda d=d: sent(d))
        guarded(diagonals[d][0], lambda d=d: to_corner(d).wait_send())
    for far in range(1, n_y):
        guarded(iy + far < n_y, lambda far=far: to_peer(far).wait_send())


def on_device(n_x, n_y, vectors, root_stiff, diag_coef, counts):
    rows, c_x, c_y, c_z = vectors.shape
    half_x, half_y = c_x // 2, c_y // 2
    vmem = pltpu.VMEM
    return pl.pallas_call(
        functools.partial(kernel, n_x, n_y),
        out_shape=(
            jax.ShapeDtypeStruct((1, 1, rows, rows), F32),
            jax.ShapeDtypeStruct((1, 1, rows, 4 * rows), F32),
            jax.ShapeDtypeStruct((1, 1, rows, 4 * rows), F32),
            jax.ShapeDtypeStruct((1, 1), jnp.int32),
        ),
        in_specs=[
            pl.BlockSpec(memory_space=pl.ANY),
            pl.BlockSpec(memory_space=pl.ANY),
            pl.BlockSpec(memory_space=pl.ANY),
            pl.BlockSpec(memory_space=pltpu.SMEM),
        ],
        out_specs=[pl.BlockSpec(memory_space=vmem)] * 4,
        scratch_shapes=[
            vmem((c_x, rows, c_y, c_z), BF16),
            vmem((c_x, c_y, c_z), F32),
            vmem((c_x, c_y, c_z), F32),
            vmem((rows * c_y, c_z), F32),
            vmem((c_x, c_y, rows, c_z), BF16),
            vmem((c_x, c_y, rows, c_z), BF16),
            vmem((c_x + 2, c_y + 2, rows, c_z), F32),
            vmem((c_y, rows, c_z), BF16),
            vmem((c_y, rows, c_z), BF16),
            vmem((c_x, rows, c_z), BF16),
            vmem((c_x, rows, c_z), BF16),
            vmem((half_y, rows, c_z), BF16),
            vmem((half_y, rows, c_z), BF16),
            vmem((half_x, rows, c_z), BF16),
            vmem((half_x, rows, c_z), BF16),
            vmem((4, rows, c_z), BF16),
            vmem((4, rows, c_z), F32),
            vmem((4, rows, c_z), F32),
            vmem((8, c_z), jnp.int32),
            vmem((n_y, 8, c_z), jnp.int32),
            pltpu.SemaphoreType.DMA((c_x + 2,)),
            pltpu.SemaphoreType.DMA((12,)),
            pltpu.SemaphoreType.DMA((12,)),
            pltpu.SemaphoreType.DMA((n_y,)),
            pltpu.SemaphoreType.DMA((n_y,)),
        ],
        compiler_params=pltpu.CompilerParams(
            collective_id=0, has_side_effects=True, vmem_limit_bytes=60 * 1024 * 1024
        ),
        cost_estimate=pl.CostEstimate(flops=600_000_000, bytes_accessed=5_000_000, transcendentals=0),
    )(vectors, root_stiff, diag_coef, counts)


def solution(mesh):
    n_x, n_y = mesh.shape["sx"], mesh.shape["sy"]
    return jax.shard_map(
        functools.partial(on_device, n_x, n_y),
        mesh=mesh,
        in_specs=(
            P(None, "sx", "sy", None),
            P("sx", "sy", None),
            P("sx", "sy", None),
            P("sx", "sy"),
        ),
        out_specs=(
            P("sx", "sy", None, None),
            P("sx", "sy", None, None),
            P("sx", "sy", None, None),
            P("sx", "sy"),
        ),
        check_vma=False,
    )
```

time: 128 us -> 43.7 us (0.34)
  the two profiles are of different devices: /device:TPU:64 before, /device:TPU:25 now
where the time goes in v1:
time: 43.7 us; the launch traced here: 43.3 us
  Pallas kernels  35.9 us (82%)
  local copies, waits for them, and re-layouts  4.32 us (10%)
  between operations  3.05 us (7%)
    pallas_call x1, Pallas kernels, on_device(): pl.pallas_call(functools.partial(kernel, n_x, n_y), out_shape=(jax.ShapeD...  35.9 us
    unnamed x3, local copies, waits for them, and re-layouts  4.32 us

profile of v1, /device:TPU:25, one launch (start us, length us, event | category | flops | bytes accessed | tf_op | source)
XLA Modules:
  0.0 43.3 jit_solution(15547801752975123961)
XLA Ops:
  1.3 35.9 %shard_map.75 = (f32[1,1,64,64]{3,2,1,0:T(8,128)}, f32[1,1,64,256]{3,2,1,0:T(8,128)}, f32[1,1,64,256]{3,2,1,0:T(8,128)}, s32[1,1]{1,0:T(1,128)}) custom-call(bf16[64,8,32,128]{3,2,1,0:T(8,128)(2,1)} %vec_ref.1, f32[8,32,128]{2,1,0:T(8,128)} %rs_ref.1, f32[8,32,128]{2,1,0:T(8,128)} %dg_ref.1, s32[1,1]{1,0:T(1,128)S(6)} %copy.12.cnt_ref), custom_call_target="tpu_custom_call" | custom-call | flops 600000000 | bytes 5000000 | tf_op jit(solution)/shard_map/pallas_call | solution.py:337
  37.2 1.4 %copy.13 = f32[1,1,64,64]{3,2,1,0:T(8,128)} copy(f32[1,1,64,64]{3,2,1,0:T(8,128)} %get-tuple-element.8) | data formatting | bytes 32768
  38.6 1.5 %copy.14 = f32[1,1,64,256]{3,2,1,0:T(8,128)} copy(f32[1,1,64,256]{3,2,1,0:T(8,128)} %get-tuple-element.9) | data formatting | bytes 131072
  40.1 1.5 %copy.15 = f32[1,1,64,256]{3,2,1,0:T(8,128)} copy(f32[1,1,64,256]{3,2,1,0:T(8,128)} %get-tuple-element.10) | data formatting | bytes 131072

commit v2 on v1

--- a/solution.py
+++ b/solution.py
@@ -10,7 +10,6 @@
 MESH = pl.DeviceIdType.MESH
 F32 = jnp.float32
 BF16 = jnp.bfloat16
-CHUNK = 4
 
 
 def row_dot(left, right):
@@ -42,14 +41,16 @@
     vv,
     rs,
     dg,
+    cnt,
     wide,
     mb,
-    sb,
+    sx0,
+    sy0,
+    sy1,
     zp,
     ab,
     vx,
     vy,
-    sy0,
     rxm,
     rxp,
     rym,
@@ -67,17 +68,21 @@
 ):
     rows, c_x, c_y, c_z = vec_ref.shape
     half_x, half_y = c_x // 2, c_y // 2
+    pitch = c_y + 1
     ix, iy = lax.axis_index("sx"), lax.axis_index("sy")
 
-    order = [0, c_x - 1] + list(range(1, c_x - 1))
-    loads = {x: pltpu.make_async_copy(vec_ref.at[:, x], vv.at[x], load_sem.at[x]) for x in order}
+    def load(x):
+        return pltpu.make_async_copy(vec_ref.at[:, x], vv.at[x], load_sem.at[x])
+
     rs_load = pltpu.make_async_copy(rs_ref, rs, load_sem.at[c_x])
     dg_load = pltpu.make_async_copy(dg_ref, dg, load_sem.at[c_x + 1])
-    loads[0].start()
+    cnt_load = pltpu.make_async_copy(cnt_ref, cnt, load_sem.at[c_x + 2])
+    cnt_load.start()
+    load(0).start()
     rs_load.start()
-    loads[c_x - 1].start()
-    for x in order[2:]:
-        loads[x].start()
+    load(c_x - 1).start()
+    for x in range(1, c_x - 1):
+        load(x).start()
     dg_load.start()
 
     low_x, high_x = ix > 0, ix < n_x - 1
@@ -111,59 +116,51 @@
     beside = sum(there.astype(jnp.int32) for there, _ in faces + diagonals)
     later = jnp.maximum(n_y - 2 - iy, 0)
 
-    count = cnt_ref[0, 0]
-    cb[...] = jnp.full(cb.shape, count, jnp.int32)
-    keep = lax.broadcasted_iota(jnp.int32, (rows, c_z), 0) < count
     lane_r = lax.broadcasted_iota(jnp.int32, (c_z, c_z), 0)
     lane_c = lax.broadcasted_iota(jnp.int32, (c_z, c_z), 1)
     apart = jnp.abs(lane_r - lane_c)
     smooth = jnp.where(apart == 0, 1.0, jnp.where(apart == 1, 0.5, 0.0)).astype(BF16)
 
-    def zero_slab(x):
-        def step(y, _):
-            zp[x, y] = jnp.zeros((rows, c_z), F32)
-            return _
-
-        lax.fori_loop(0, c_y + 2, step, 0)
-
-    zero_slab(0)
-    zero_slab(c_x + 1)
+    def zero_row(y, _):
+        zp[0, y] = jnp.zeros((rows, c_z), F32)
+        zp[c_x + 1, y] = jnp.zeros((rows, c_z), F32)
+        return _
+
+    lax.fori_loop(0, c_y + 2, zero_row, 0)
     for x in range(1, c_x + 1):
         zp[x, 0] = jnp.zeros((rows, c_z), F32)
         zp[x, c_y + 1] = jnp.zeros((rows, c_z), F32)
 
-    def widen(x):
-        wide[...] = vv[x].reshape(rows * c_y, c_z).astype(F32)
-
-    def scale(x):
-        def step(i, _):
-            pieces = []
-            for j in range(CHUNK):
-                y = i * CHUNK + j
-                m = wide[pl.ds(y, rows, stride=c_y), :]
-                m = jnp.where(keep, m, 0.0)
-                s = (m * rs[x, pl.ds(y, 1), :]).astype(BF16)
-                mb[x, y] = m.astype(BF16)
-                sb[x, y] = s
-                pieces.append(s)
-            z = jnp.dot(jnp.concatenate(pieces, axis=0), smooth, preferred_element_type=F32)
-            for j in range(CHUNK):
-                zp[x + 1, i * CHUNK + j + 1] = z[j * rows : (j + 1) * rows]
-            return _
-
-        lax.fori_loop(0, c_y // CHUNK, step, 0)
+    cnt_load.wait()
+    cb[...] = jnp.broadcast_to(cnt[...], cb.shape)
+    keep = lax.broadcasted_iota(jnp.int32, (rows, c_z), 0) < cnt[...]
+
+    def scale(x, edge=False):
+        load(x).wait()
+        for a in range(rows):
+            wide[a * pitch : a * pitch + c_y, :] = vv[x, a].astype(F32)
+        pieces = []
+        for y in range(c_y):
+            m = jnp.where(keep, wide[pl.ds(y, rows, stride=pitch), :], 0.0)
+            s = (m * rs[x, y : y + 1, :]).astype(BF16)
+            mb[x, y] = m.astype(BF16)
+            if edge:
+                sx0[y] = s
+            if y == 0:
+                sy0[x] = s
+            if y == c_y - 1:
+                sy1[x] = s
+            pieces.append(s)
+        z = jnp.dot(jnp.concatenate(pieces, axis=0), smooth, preferred_element_type=F32)
+        for y in range(c_y):
+            zp[x + 1, y + 1] = z[y * rows : (y + 1) * rows]
 
     rs_load.wait()
-    for x in (0, c_x - 1):
-        loads[x].wait()
-        widen(x)
-        scale(x)
-
-    def face_step(y, _):
+    scale(0, True)
+    scale(c_x - 1)
+
+    for y in range(c_y):
         vx[y] = (-0.25 * ((zp[c_x, y] + zp[c_x, y + 2]) + 2.0 * zp[c_x, y + 1])).astype(BF16)
-        return _
-
-    lax.fori_loop(0, c_y, face_step, 0)
 
     pl.semaphore_wait(barrier, beside + later)
 
@@ -171,7 +168,7 @@
         opposite = d ^ 1
         if phase == 0:
             src, dst = [
-                (sb.at[0, pl.ds(0, half_y)], rxp),
+                (sx0.at[pl.ds(0, half_y)], rxp),
                 (vx.at[pl.ds(half_y, half_y)], rxm),
                 (sy0.at[pl.ds(0, half_x)], ryp),
                 (vy.at[pl.ds(half_x, half_x)], rym),
@@ -187,23 +184,23 @@
             device_id_type=MESH,
         )
 
-    def from_face(d, phase):
-        return to_face(d ^ 1, phase, d)
-
-    def from_corner(d):
-        return to_corner(3 - d, d)
-
     def to_corner(d, to=None):
         opposite = 3 - d
-        x, y = (0, c_x - 1)[d // 2], (0, c_y - 1)[d % 2]
+        side = (sy0, sy1)[d % 2]
         return pltpu.make_async_remote_copy(
-            src_ref=sb.at[x, y],
+            src_ref=side.at[(0, c_x - 1)[d // 2]],
             dst_ref=rc.at[opposite],
             send_sem=send_sem.at[8 + d],
             recv_sem=recv_sem.at[8 + opposite],
             device_id=diagonals[d if to is None else to][1],
             device_id_type=MESH,
         )
+
+    def from_face(d, phase):
+        return to_face(d ^ 1, phase, d)
+
+    def from_corner(d):
+        return to_corner(3 - d, d)
 
     def to_peer(far):
         return pltpu.make_async_remote_copy(
@@ -227,16 +224,14 @@
     for far in range(1, n_y):
         guarded(iy + far < n_y, lambda far=far: to_peer(far).start())
 
-    for x in order[2:]:
-        loads[x].wait()
-        widen(x)
+    def scale_step(x, _):
         scale(x)
+        return _
+
+    lax.fori_loop(1, c_x - 1, scale_step, 0)
 
     for x in range(c_x):
-        vy[x] = (
-            -0.25 * ((zp[x, c_y] + zp[x + 2, c_y]) + 2.0 * zp[x + 1, c_y])
-        ).astype(BF16)
-        sy0[x] = sb[x, 0]
+        vy[x] = (-0.25 * ((zp[x, c_y] + zp[x + 2, c_y]) + 2.0 * zp[x + 1, c_y])).astype(BF16)
     for d in (3, 2):
         guarded(faces[d][0], lambda d=d: to_face(d, 0).start())
 
@@ -244,43 +239,50 @@
     dg[...] = dg[...] + rs[...] * rs[...]
     rs[...] = rs[...] * 0.25
 
-    def apply_slab(x, total):
+    def apply(x, slot):
         def across(y):
             near = zp[x + 1, y]
             return (zp[x, y] + near) + (near + zp[x + 2, y])
 
-        def step(i, carry):
-            g_here, u_before, total = carry
-            for j in range(CHUNK):
-                y = i * CHUNK + j
-                g_next = across(y + 2)
-                u_after = g_here + g_next
-                q = u_before + u_after
-                m = mb[x, y].astype(F32)
-                applied = dg[x, pl.ds(y, 1), :] * m - rs[x, pl.ds(y, 1), :] * q
-                ab[y] = applied.astype(BF16)
-                g_here, u_before = g_next, u_after
-            left = along_lanes([mb[x, i * CHUNK + j] for j in range(CHUNK)])
-            right = along_lanes([ab[i * CHUNK + j] for j in range(CHUNK)])
-            return g_here, u_before, total + row_dot(left, right)
-
-        first = across(1)
-        carry = lax.fori_loop(0, c_y // CHUNK, step, (first, first, total))
-        return carry[2]
-
-    own_ref[0, 0] = lax.fori_loop(0, c_x, apply_slab, jnp.zeros((rows, rows), F32))
+        here = across(1)
+        before = here
+        for y in range(c_y):
+            ahead = across(y + 2)
+            after = here + ahead
+            m = mb[x, y].astype(F32)
+            applied = dg[x, pl.ds(y, 1), :] * m - rs[x, pl.ds(y, 1), :] * (before + after)
+            ab[slot, y] = applied.astype(BF16)
+            here, before = ahead, after
+
+    def product(x, slot):
+        return block_dot(mb.at[x], 0, ab.at[slot], 0, c_y)
+
+    apply(0, 0)
+
+    def own_step(i, total):
+        x = 2 * i
+        total = total + product(x, 0)
+        apply(x + 1, 1)
+        total = total + product(x + 1, 1)
+        apply(x + 2, 0)
+        return total
+
+    total = lax.fori_loop(0, c_x // 2 - 1, own_step, jnp.zeros((rows, rows), F32))
+    total = total + product(c_x - 2, 0)
+    apply(c_x - 1, 1)
+    own_ref[0, 0] = total + product(c_x - 1, 1)
 
     def half_sum(d):
         from_face(d, 0).wait_recv()
         mine, mine_at, other, depth = [
-            (sb.at[0], half_y, rxm, half_y),
+            (sx0, half_y, rxm, half_y),
             (vx, 0, rxp, half_y),
             (sy0, half_x, rym, half_x),
             (vy, 0, ryp, half_x),
         ][d]
-        face_ref[0, 0, :, d * rows : (d + 1) * rows] = block_dot(mine, mine_at, other, 0, depth)
         pout[d, :, 0:rows] = block_dot(other, 0, mine, mine_at, depth)
         to_face(d, 1).start()
+        face_ref[0, 0, :, d * rows : (d + 1) * rows] = block_dot(mine, mine_at, other, 0, depth)
 
     for d in (2, 3, 0, 1):
         guarded(faces[d][0], lambda d=d: half_sum(d))
@@ -330,36 +332,44 @@
         guarded(iy + far < n_y, lambda far=far: to_peer(far).wait_send())
 
 
+def hand_on(*refs):
+    n = (len(refs) - 1) // 2
+    copies = [pltpu.make_async_copy(refs[i], refs[n + i], refs[-1].at[i]) for i in range(n)]
+    for copy in copies:
+        copy.start()
+    for copy in copies:
+        copy.wait()
+
+
 def on_device(n_x, n_y, vectors, root_stiff, diag_coef, counts):
     rows, c_x, c_y, c_z = vectors.shape
     half_x, half_y = c_x // 2, c_y // 2
     vmem = pltpu.VMEM
-    return pl.pallas_call(
+    results = (
+        jax.ShapeDtypeStruct((1, 1, rows, rows), F32),
+        jax.ShapeDtypeStruct((1, 1, rows, 4 * rows), F32),
+        jax.ShapeDtypeStruct((1, 1, rows, 4 * rows), F32),
+        jax.ShapeDtypeStruct((1, 1), jnp.int32),
+    )
+    anywhere = pl.BlockSpec(memory_space=pl.ANY)
+    outputs = pl.pallas_call(
         functools.partial(kernel, n_x, n_y),
-        out_shape=(
-            jax.ShapeDtypeStruct((1, 1, rows, rows), F32),
-            jax.ShapeDtypeStruct((1, 1, rows, 4 * rows), F32),
-            jax.ShapeDtypeStruct((1, 1, rows, 4 * rows), F32),
-            jax.ShapeDtypeStruct((1, 1), jnp.int32),
-        ),
-        in_specs=[
-            pl.BlockSpec(memory_space=pl.ANY),
-            pl.BlockSpec(memory_space=pl.ANY),
-            pl.BlockSpec(memory_space=pl.ANY),
-            pl.BlockSpec(memory_space=pltpu.SMEM),
-        ],
+        out_shape=results,
+        in_specs=[anywhere] * 3 + [pl.BlockSpec(memory_space=pltpu.HBM)],
         out_specs=[pl.BlockSpec(memory_space=vmem)] * 4,
         scratch_shapes=[
             vmem((c_x, rows, c_y, c_z), BF16),
             vmem((c_x, c_y, c_z), F32),
             vmem((c_x, c_y, c_z), F32),
-            vmem((rows * c_y, c_z), F32),
+            vmem((1, 1), jnp.int32),
+            vmem((rows * (c_y + 1) + 7, c_z), F32),
             vmem((c_x, c_y, rows, c_z), BF16),
-            vmem((c_x, c_y, rows, c_z), BF16),
-            vmem((c_x + 2, c_y + 2, rows, c_z), F32),
-            vmem((c_y, rows, c_z), BF16),
             vmem((c_y, rows, c_z), BF16),
             vmem((c_x, rows, c_z), BF16),
+            vmem((c_x, rows, c_z), BF16),
+            vmem((c_x + 2, c_y + 2, rows, c_z), F32),
+            vmem((2, c_y, rows, c_z), BF16),
+            vmem((c_y, rows, c_z), BF16),
             vmem((c_x, rows, c_z), BF16),
             vmem((half_y, rows, c_z), BF16),
             vmem((half_y, rows, c_z), BF16),
@@ -370,7 +380,7 @@
             vmem((4, rows, c_z), F32),
             vmem((8, c_z), jnp.int32),
             vmem((n_y, 8, c_z), jnp.int32),
-            pltpu.SemaphoreType.DMA((c_x + 2,)),
+            pltpu.SemaphoreType.DMA((c_x + 3,)),
             pltpu.SemaphoreType.DMA((12,)),
             pltpu.SemaphoreType.DMA((12,)),
             pltpu.SemaphoreType.DMA((n_y,)),
@@ -380,7 +390,16 @@
             collective_id=0, has_side_effects=True, vmem_limit_bytes=60 * 1024 * 1024
         ),
         cost_estimate=pl.CostEstimate(flops=600_000_000, bytes_accessed=5_000_000, transcendentals=0),
+        name="coarse",
     )(vectors, root_stiff, diag_coef, counts)
+    return pl.pallas_call(
+        hand_on,
+        out_shape=results,
+        in_specs=[anywhere] * len(results),
+        out_specs=[anywhere] * len(results),
+        scratch_shapes=[pltpu.SemaphoreType.DMA((len(results),))],
+        name="results",
+    )(*outputs)
 
 
 def solution(mesh):

time: 43.7 us -> 27.8 us (0.64)
  the two profiles are of different devices: /device:TPU:25 before, /device:TPU:2 now
where the time goes in v2:
time: 27.8 us; the launch traced here: 27.7 us
  Pallas kernels  26.4 us (95%)
  between operations  1.29 us (5%)
    pallas_call x1, Pallas kernels, on_device(): pl.pallas_call(functools.partial(kernel, n_x, n_y), out_shape=results, in...  19.7 us
    pallas_call x1, Pallas kernels, on_device(): pl.pallas_call(hand_on, out_shape=results, in_specs=[anywhere] * len(resu...  6.73 us

profile of v2, /device:TPU:2, one launch (start us, length us, event | category | flops | bytes accessed | tf_op | source)
XLA Modules:
  0.0 27.7 jit_solution(2274889220397431522)
XLA Ops:
  1.3 19.7 %coarse.1 = (f32[1,1,64,64]{3,2,1,0:T(8,128)}, f32[1,1,64,256]{3,2,1,0:T(8,128)}, f32[1,1,64,256]{3,2,1,0:T(8,128)}, s32[1,1]{1,0:T(1,128)}) custom-call(bf16[64,8,32,128]{3,2,1,0:T(8,128)(2,1)} %vec_ref.1, f32[8,32,128]{2,1,0:T(8,128)} %rs_ref.1, f32[8,32,128]{2,1,0:T(8,128)} %dg_ref.1, s32[1,1]{1,0:T(1,128)S(6)} %copy.8.cnt_ref), custom_call_target="tpu_custom_call" | custom-call | flops 600000000 | bytes 5000000 | tf_op jit(solution)/shard_map/coarse/pallas_call | solution.py:355
  21.0 6.7 %results.1 = (f32[1,1,64,64]{3,2,1,0:T(8,128)}, f32[1,1,64,256]{3,2,1,0:T(8,128)}, f32[1,1,64,256]{3,2,1,0:T(8,128)}, s32[1,1]{1,0:T(1,128)}) custom-call(f32[1,1,64,64]{3,2,1,0:T(8,128)} %get-tuple-element.8.refs_0_, f32[1,1,64,256]{3,2,1,0:T(8,128)} %get-tuple-element.9.refs_1_, f32[1,1,64,256]{3,2,1,0:T(8,128)} %get-tuple-element.10.refs_2_, ...), custom_call_target="tpu_custom_call" | custom-call | tf_op jit(solution)/shard_map/results/pallas_call | solution.py:395

commit v3 on v2

--- a/solution.py
+++ b/solution.py
@@ -44,17 +44,16 @@
     cnt,
     wide,
     mb,
-    sx0,
+    sx,
     sy0,
     sy1,
+    lean,
     zp,
     ab,
     vx,
     vy,
-    rxm,
-    rxp,
-    rym,
-    ryp,
+    rx,
+    ry,
     rc,
     pout,
     pin,
@@ -67,7 +66,7 @@
     crecv_sem,
 ):
     rows, c_x, c_y, c_z = vec_ref.shape
-    half_x, half_y = c_x // 2, c_y // 2
+    half_x = c_x // 2
     pitch = c_y + 1
     ix, iy = lax.axis_index("sx"), lax.axis_index("sy")
 
@@ -135,32 +134,48 @@
     cb[...] = jnp.broadcast_to(cnt[...], cb.shape)
     keep = lax.broadcasted_iota(jnp.int32, (rows, c_z), 0) < cnt[...]
 
-    def scale(x, edge=False):
+    def widen(x):
         load(x).wait()
         for a in range(rows):
-            wide[a * pitch : a * pitch + c_y, :] = vv[x, a].astype(F32)
+            wide[x, a * pitch : a * pitch + c_y, :] = vv[x, a].astype(F32)
+
+    def row(x, y):
+        m = jnp.where(keep, wide[x, pl.ds(y, rows, stride=pitch), :], 0.0)
+        return m, m * rs[x, y : y + 1, :]
+
+    def scale(x, side=None):
         pieces = []
         for y in range(c_y):
-            m = jnp.where(keep, wide[pl.ds(y, rows, stride=pitch), :], 0.0)
-            s = (m * rs[x, y : y + 1, :]).astype(BF16)
+            m, s = row(x, y)
+            s = s.astype(BF16)
             mb[x, y] = m.astype(BF16)
-            if edge:
-                sx0[y] = s
-            if y == 0:
-                sy0[x] = s
-            if y == c_y - 1:
-                sy1[x] = s
+            if side is not None:
+                sx[side, y] = s
             pieces.append(s)
         z = jnp.dot(jnp.concatenate(pieces, axis=0), smooth, preferred_element_type=F32)
         for y in range(c_y):
             zp[x + 1, y + 1] = z[y * rows : (y + 1) * rows]
 
     rs_load.wait()
-    scale(0, True)
-    scale(c_x - 1)
-
-    for y in range(c_y):
-        vx[y] = (-0.25 * ((zp[c_x, y] + zp[c_x, y + 2]) + 2.0 * zp[c_x, y + 1])).astype(BF16)
+    widen(0)
+    scale(0, 0)
+    widen(c_x - 1)
+    scale(c_x - 1, 1)
+
+    def widen_step(x, _):
+        widen(x)
+        return _
+
+    lax.fori_loop(1, c_x - 1, widen_step, 0)
+    ends = []
+    for x in range(c_x):
+        sy0[x] = row(x, 0)[1].astype(BF16)
+        s = row(x, c_y - 1)[1]
+        sy1[x] = s.astype(BF16)
+        ends.append(s)
+    ends.append(jnp.zeros((rows, c_z), F32))
+    for x in range(half_x, c_x):
+        lean[x - half_x] = (ends[x] + 0.5 * (ends[x - 1] + ends[x + 1])).astype(BF16)
 
     pl.semaphore_wait(barrier, beside + later)
 
@@ -168,13 +183,13 @@
         opposite = d ^ 1
         if phase == 0:
             src, dst = [
-                (sx0.at[pl.ds(0, half_y)], rxp),
-                (vx.at[pl.ds(half_y, half_y)], rxm),
-                (sy0.at[pl.ds(0, half_x)], ryp),
-                (vy.at[pl.ds(half_x, half_x)], rym),
+                (sx.at[0], rx.at[1]),
+                (sx.at[1], rx.at[0]),
+                (sy0.at[pl.ds(0, half_x)], ry.at[1]),
+                (lean, ry.at[0]),
             ][d]
         else:
-            src, dst = pout.at[d], pin.at[opposite]
+            src, dst = pout.at[d - 2], pin.at[opposite - 2]
         return pltpu.make_async_remote_copy(
             src_ref=src,
             dst_ref=dst,
@@ -217,7 +232,7 @@
         def _():
             action()
 
-    for d in (1, 0):
+    for d in (3, 2, 1, 0):
         guarded(faces[d][0], lambda d=d: to_face(d, 0).start())
     for d in range(4):
         guarded(diagonals[d][0], lambda d=d: to_corner(d).start())
@@ -230,10 +245,16 @@
 
     lax.fori_loop(1, c_x - 1, scale_step, 0)
 
-    for x in range(c_x):
-        vy[x] = (-0.25 * ((zp[x, c_y] + zp[x + 2, c_y]) + 2.0 * zp[x + 1, c_y])).astype(BF16)
-    for d in (3, 2):
-        guarded(faces[d][0], lambda d=d: to_face(d, 0).start())
+    for side, x in enumerate((1, c_x)):
+        for y in range(c_y):
+            vx[side, y] = (
+                -0.25 * ((zp[x, y] + zp[x, y + 2]) + 2.0 * zp[x, y + 1])
+            ).astype(BF16)
+    for x in range(half_x):
+        vy[0, x] = (-0.5 * zp[half_x + x + 1, 1]).astype(BF16)
+        vy[1, x] = (
+            -0.25 * ((zp[x, c_y] + zp[x + 2, c_y]) + 2.0 * zp[x + 1, c_y])
+        ).astype(BF16)
 
     dg_load.wait()
     dg[...] = dg[...] + rs[...] * rs[...]
@@ -267,25 +288,21 @@
         apply(x + 2, 0)
         return total
 
-    total = lax.fori_loop(0, c_x // 2 - 1, own_step, jnp.zeros((rows, rows), F32))
+    def half_sum(d):
+        from_face(d, 0).wait_recv()
+        mine, other = vy.at[d - 2], ry.at[d - 2]
+        pout[d - 2, :, 0:rows] = block_dot(other, 0, mine, 0, half_x)
+        to_face(d, 1).start()
+        face_ref[0, 0, :, d * rows : (d + 1) * rows] = block_dot(mine, 0, other, 0, half_x)
+
+    steps = c_x // 2 - 1
+    total = lax.fori_loop(0, steps - 1, own_step, jnp.zeros((rows, rows), F32))
+    for d in (2, 3):
+        guarded(faces[d][0], lambda d=d: half_sum(d))
+    total = lax.fori_loop(steps - 1, steps, own_step, total)
     total = total + product(c_x - 2, 0)
     apply(c_x - 1, 1)
     own_ref[0, 0] = total + product(c_x - 1, 1)
-
-    def half_sum(d):
-        from_face(d, 0).wait_recv()
-        mine, mine_at, other, depth = [
-            (sx0, half_y, rxm, half_y),
-            (vx, 0, rxp, half_y),
-            (sy0, half_x, rym, half_x),
-            (vy, 0, ryp, half_x),
-        ][d]
-        pout[d, :, 0:rows] = block_dot(other, 0, mine, mine_at, depth)
-        to_face(d, 1).start()
-        face_ref[0, 0, :, d * rows : (d + 1) * rows] = block_dot(mine, mine_at, other, 0, depth)
-
-    for d in (2, 3, 0, 1):
-        guarded(faces[d][0], lambda d=d: half_sum(d))
 
     for d in range(4):
 
@@ -310,20 +327,25 @@
 
         guarded(iy >= far, earlier)
 
-    def finish(d):
+    def finish_y(d):
         from_face(d, 1).wait_recv()
-        face_ref[0, 0, :, d * rows : (d + 1) * rows] += pin[d, :, 0:rows]
+        face_ref[0, 0, :, d * rows : (d + 1) * rows] += pin[d - 2, :, 0:rows]
+
+    def finish_x(d):
+        from_face(d, 0).wait_recv()
+        face_ref[0, 0, :, d * rows : (d + 1) * rows] = block_dot(vx.at[d], 0, rx.at[d], 0, c_y)
 
     def face_zero(d):
         face_ref[0, 0, :, d * rows : (d + 1) * rows] = jnp.zeros((rows, rows), F32)
 
     for d in (2, 3, 0, 1):
-        guarded(faces[d][0], lambda d=d: finish(d))
+        guarded(faces[d][0], lambda d=d: (finish_x if d < 2 else finish_y)(d))
         guarded(jnp.logical_not(faces[d][0]), lambda d=d: face_zero(d))
 
     def sent(d):
         to_face(d, 0).wait_send()
-        to_face(d, 1).wait_send()
+        if d >= 2:
+            to_face(d, 1).wait_send()
 
     for d in range(4):
         guarded(faces[d][0], lambda d=d: sent(d))
@@ -333,17 +355,14 @@
 
 
 def hand_on(*refs):
-    n = (len(refs) - 1) // 2
-    copies = [pltpu.make_async_copy(refs[i], refs[n + i], refs[-1].at[i]) for i in range(n)]
-    for copy in copies:
-        copy.start()
-    for copy in copies:
-        copy.wait()
+    n = len(refs) // 2
+    for i in range(n):
+        refs[n + i][...] = refs[i][...]
 
 
 def on_device(n_x, n_y, vectors, root_stiff, diag_coef, counts):
     rows, c_x, c_y, c_z = vectors.shape
-    half_x, half_y = c_x // 2, c_y // 2
+    half_x = c_x // 2
     vmem = pltpu.VMEM
     results = (
         jax.ShapeDtypeStruct((1, 1, rows, rows), F32),
@@ -362,22 +381,21 @@
             vmem((c_x, c_y, c_z), F32),
             vmem((c_x, c_y, c_z), F32),
             vmem((1, 1), jnp.int32),
-            vmem((rows * (c_y + 1) + 7, c_z), F32),
+            vmem((c_x, rows * (c_y + 1) + 7, c_z), F32),
             vmem((c_x, c_y, rows, c_z), BF16),
-            vmem((c_y, rows, c_z), BF16),
+            vmem((2, c_y, rows, c_z), BF16),
             vmem((c_x, rows, c_z), BF16),
             vmem((c_x, rows, c_z), BF16),
+            vmem((half_x, rows, c_z), BF16),
             vmem((c_x + 2, c_y + 2, rows, c_z), F32),
             vmem((2, c_y, rows, c_z), BF16),
-            vmem((c_y, rows, c_z), BF16),
-            vmem((c_x, rows, c_z), BF16),
-            vmem((half_y, rows, c_z), BF16),
-            vmem((half_y, rows, c_z), BF16),
-            vmem((half_x, rows, c_z), BF16),
-            vmem((half_x, rows, c_z), BF16),
+            vmem((2, c_y, rows, c_z), BF16),
+            vmem((2, half_x, rows, c_z), BF16),
+            vmem((2, c_y, rows, c_z), BF16),
+            vmem((2, half_x, rows, c_z), BF16),
             vmem((4, rows, c_z), BF16),
-            vmem((4, rows, c_z), F32),
-            vmem((4, rows, c_z), F32),
+            vmem((2, rows, c_z), F32),
+            vmem((2, rows, c_z), F32),
             vmem((8, c_z), jnp.int32),
             vmem((n_y, 8, c_z), jnp.int32),
             pltpu.SemaphoreType.DMA((c_x + 3,)),
@@ -395,9 +413,8 @@
     return pl.pallas_call(
         hand_on,
         out_shape=results,
-        in_specs=[anywhere] * len(results),
-        out_specs=[anywhere] * len(results),
-        scratch_shapes=[pltpu.SemaphoreType.DMA((len(results),))],
+        in_specs=[pl.BlockSpec(memory_space=vmem)] * len(results),
+        out_specs=[pl.BlockSpec(memory_space=vmem)] * len(results),
         name="results",
     )(*outputs)
 

time: 27.8 us -> 24.7 us (0.89)
  Pallas kernels: 26.4 us -> 23.2 us
    pallas_call x1, Pallas kernels: 6.73 us -> 2.19 us  [on_device(): pl.pallas_call(hand_on, out_shape=results, in_specs=[pl.BlockSpec(memory_...]
    pallas_call x1, Pallas kernels: 19.7 us -> 21 us  [on_device(): pl.pallas_call(functools.partial(kernel, n_x, n_y), out_shape=results, in...]
where the time goes in v3:
time: 24.7 us; the launch traced here: 24.5 us
  Pallas kernels  23.2 us (94%)
  between operations  1.29 us (5%)
    pallas_call x1, Pallas kernels, on_device(): pl.pallas_call(functools.partial(kernel, n_x, n_y), out_shape=results, in...  21 us
    pallas_call x1, Pallas kernels, on_device(): pl.pallas_call(hand_on, out_shape=results, in_specs=[pl.BlockSpec(memory_...  2.19 us

profile of v3, /device:TPU:2, one launch (start us, length us, event | category | flops | bytes accessed | tf_op | source)
XLA Modules:
  0.0 24.5 jit_solution(12911774150496587336)
XLA Ops:
  1.3 21.0 %coarse.1 = (f32[1,1,64,64]{3,2,1,0:T(8,128)}, f32[1,1,64,256]{3,2,1,0:T(8,128)}, f32[1,1,64,256]{3,2,1,0:T(8,128)}, s32[1,1]{1,0:T(1,128)}) custom-call(bf16[64,8,32,128]{3,2,1,0:T(8,128)(2,1)} %vec_ref.1, f32[8,32,128]{2,1,0:T(8,128)} %rs_ref.1, f32[8,32,128]{2,1,0:T(8,128)} %dg_ref.1, s32[1,1]{1,0:T(1,128)S(6)} %copy.8.cnt_ref), custom_call_target="tpu_custom_call" | custom-call | flops 600000000 | bytes 5000000 | tf_op jit(solution)/shard_map/coarse/pallas_call | solution.py:374
  22.3 2.2 %results.1 = (f32[1,1,64,64]{3,2,1,0:T(8,128)}, f32[1,1,64,256]{3,2,1,0:T(8,128)}, f32[1,1,64,256]{3,2,1,0:T(8,128)}, s32[1,1]{1,0:T(1,128)}) custom-call(f32[1,1,64,64]{3,2,1,0:T(8,128)} %get-tuple-element.8.refs_0_, f32[1,1,64,256]{3,2,1,0:T(8,128)} %get-tuple-element.9.refs_1_, f32[1,1,64,256]{3,2,1,0:T(8,128)} %get-tuple-element.10.refs_2_, ...), custom_call_target="tpu_custom_call" | custom-call | tf_op jit(solution)/shard_map/results/pallas_call | solution.py:413

commit v4 on v3

--- a/solution.py
+++ b/solution.py
@@ -47,7 +47,6 @@
     sx,
     sy0,
     sy1,
-    lean,
     zp,
     ab,
     vx,
@@ -55,18 +54,19 @@
     rx,
     ry,
     rc,
-    pout,
-    pin,
+    rr,
     cb,
+    cb_last,
     cr,
     load_sem,
     send_sem,
     recv_sem,
     csend_sem,
     crecv_sem,
+    relay_sem,
 ):
     rows, c_x, c_y, c_z = vec_ref.shape
-    half_x = c_x // 2
+    rounds = cb.shape[0]
     pitch = c_y + 1
     ix, iy = lax.axis_index("sx"), lax.axis_index("sy")
 
@@ -106,14 +106,25 @@
         def _(device=device):
             pl.semaphore_signal(barrier, inc=1, device_id=device, device_id_type=MESH)
 
-    for far in range(2, n_y):
-
-        @pl.when(iy >= far)
-        def _(far=far):
-            pl.semaphore_signal(barrier, inc=1, device_id=(ix, iy - far), device_id_type=MESH)
-
-    beside = sum(there.astype(jnp.int32) for there, _ in faces + diagonals)
-    later = jnp.maximum(n_y - 2 - iy, 0)
+    across_low, across_high = n_x // 2 - 1, n_x // 2
+    is_origin = (ix == across_low) | (ix == across_high)
+    is_relay = (ix == 0) | (ix == n_x - 1)
+    via_y = iy + 1 - 2 * lax.rem(iy, 2)
+    origin_to = (jnp.where(ix == across_low, n_x - 1, 0), via_y)
+    relay_to = (jnp.where(ix == 0, across_low, across_high), via_y)
+    relay_from = (jnp.where(ix == 0, across_high, across_low), via_y)
+    target_from = (jnp.where(ix == across_low, 0, n_x - 1), via_y)
+
+    @pl.when(is_relay)
+    def _():
+        pl.semaphore_signal(barrier, inc=1, device_id=relay_from, device_id_type=MESH)
+
+    @pl.when(is_origin)
+    def _():
+        pl.semaphore_signal(barrier, inc=1, device_id=target_from, device_id_type=MESH)
+
+    greeted = sum(there.astype(jnp.int32) for there, _ in faces + diagonals)
+    greeted = greeted + (is_relay | is_origin).astype(jnp.int32)
 
     lane_r = lax.broadcasted_iota(jnp.int32, (c_z, c_z), 0)
     lane_c = lax.broadcasted_iota(jnp.int32, (c_z, c_z), 1)
@@ -131,7 +142,7 @@
         zp[x, c_y + 1] = jnp.zeros((rows, c_z), F32)
 
     cnt_load.wait()
-    cb[...] = jnp.broadcast_to(cnt[...], cb.shape)
+    cb[0] = jnp.broadcast_to(cnt[...], cb.shape[1:])
     keep = lax.broadcasted_iota(jnp.int32, (rows, c_z), 0) < cnt[...]
 
     def widen(x):
@@ -167,35 +178,44 @@
         return _
 
     lax.fori_loop(1, c_x - 1, widen_step, 0)
-    ends = []
     for x in range(c_x):
         sy0[x] = row(x, 0)[1].astype(BF16)
-        s = row(x, c_y - 1)[1]
-        sy1[x] = s.astype(BF16)
-        ends.append(s)
-    ends.append(jnp.zeros((rows, c_z), F32))
-    for x in range(half_x, c_x):
-        lean[x - half_x] = (ends[x] + 0.5 * (ends[x - 1] + ends[x + 1])).astype(BF16)
-
-    pl.semaphore_wait(barrier, beside + later)
-
-    def to_face(d, phase, to=None):
+        sy1[x] = row(x, c_y - 1)[1].astype(BF16)
+
+    pl.semaphore_wait(barrier, greeted)
+
+    def to_face(d, part, to=None):
         opposite = d ^ 1
-        if phase == 0:
-            src, dst = [
-                (sx.at[0], rx.at[1]),
-                (sx.at[1], rx.at[0]),
-                (sy0.at[pl.ds(0, half_x)], ry.at[1]),
-                (lean, ry.at[0]),
-            ][d]
+        if d < 2:
+            piece = pl.ds(part * (c_y // 2), c_y // 2)
+            src, dst = sx.at[d, piece], rx.at[opposite, piece]
         else:
-            src, dst = pout.at[d - 2], pin.at[opposite - 2]
+            src, dst = (sy0, sy1)[d - 2], ry.at[opposite - 2]
         return pltpu.make_async_remote_copy(
             src_ref=src,
             dst_ref=dst,
-            send_sem=send_sem.at[phase * 4 + d],
-            recv_sem=recv_sem.at[phase * 4 + opposite],
+            send_sem=send_sem.at[part * 2 + d if d < 2 else 2 + d],
+            recv_sem=recv_sem.at[part * 2 + opposite if d < 2 else 2 + opposite],
             device_id=faces[d if to is None else to][1],
+            device_id_type=MESH,
+        )
+
+    def from_face(d, part):
+        return to_face(d ^ 1, part, d)
+
+    def by_relay(d, leg, chunk):
+        opposite = d ^ 1
+        piece = pl.ds(c_y // 2 + chunk * (c_y // 4), c_y // 4)
+        src, dst = [
+            (sx.at[d, piece], rr.at[chunk]),
+            (rr.at[chunk], rx.at[opposite, piece]),
+        ][leg]
+        return pltpu.make_async_remote_copy(
+            src_ref=src,
+            dst_ref=dst,
+            send_sem=relay_sem.at[0, leg, chunk],
+            recv_sem=relay_sem.at[1, leg, chunk],
+            device_id=(origin_to, relay_to)[leg],
             device_id_type=MESH,
         )
 
@@ -211,19 +231,17 @@
             device_id_type=MESH,
         )
 
-    def from_face(d, phase):
-        return to_face(d ^ 1, phase, d)
-
     def from_corner(d):
         return to_corner(3 - d, d)
 
-    def to_peer(far):
+    def to_peer(r, up):
+        far = 2**r
         return pltpu.make_async_remote_copy(
-            src_ref=cb,
-            dst_ref=cr.at[far],
-            send_sem=csend_sem.at[far],
-            recv_sem=crecv_sem.at[far],
-            device_id=(ix, iy + far),
+            src_ref=cb.at[r],
+            dst_ref=cr.at[r, up],
+            send_sem=csend_sem.at[r, up],
+            recv_sem=crecv_sem.at[r, up],
+            device_id=(ix, iy + far if up else iy - far),
             device_id_type=MESH,
         )
 
@@ -232,12 +250,46 @@
         def _():
             action()
 
-    for d in (3, 2, 1, 0):
+    def origin_of(d):
+        return ix == (across_high, across_low)[d]
+
+    def send_x(d):
+        @pl.when(origin_of(d))
+        def _():
+            for chunk in range(2):
+                by_relay(d, 0, chunk).start()
+
+        @pl.when(jnp.logical_not(origin_of(d)))
+        def _():
+            to_face(d, 1).start()
+
+        to_face(d, 0).start()
+
+    def send_counts(r):
+        guarded(iy + 2**r < n_y, lambda: to_peer(r, 1).start())
+        if r + 1 < rounds:
+            guarded(iy >= 2**r, lambda: to_peer(r, 0).start())
+
+    def add_counts(r):
+        far = 2**r
+        cb_next = cb.at[r + 1] if r + 1 < rounds else cb_last
+        cb_next[...] = cb[r]
+
+        @pl.when(iy >= far)
+        def _():
+            to_peer(r, 1).wait_recv()
+            cb_next[...] += cr[r, 1]
+
+        if r + 1 < rounds:
+            guarded(iy + far < n_y, lambda: to_peer(r, 0).wait_recv())
+
+    send_counts(0)
+    for d in (1, 0):
+        guarded(faces[d][0], lambda d=d: send_x(d))
+    for d in (3, 2):
         guarded(faces[d][0], lambda d=d: to_face(d, 0).start())
     for d in range(4):
         guarded(diagonals[d][0], lambda d=d: to_corner(d).start())
-    for far in range(1, n_y):
-        guarded(iy + far < n_y, lambda far=far: to_peer(far).start())
 
     def scale_step(x, _):
         scale(x)
@@ -250,11 +302,11 @@
             vx[side, y] = (
                 -0.25 * ((zp[x, y] + zp[x, y + 2]) + 2.0 * zp[x, y + 1])
             ).astype(BF16)
-    for x in range(half_x):
-        vy[0, x] = (-0.5 * zp[half_x + x + 1, 1]).astype(BF16)
-        vy[1, x] = (
-            -0.25 * ((zp[x, c_y] + zp[x + 2, c_y]) + 2.0 * zp[x + 1, c_y])
-        ).astype(BF16)
+    for side, y in enumerate((1, c_y)):
+        for x in range(c_x):
+            vy[side, x] = (
+                -0.25 * ((zp[x, y] + zp[x + 2, y]) + 2.0 * zp[x + 1, y])
+            ).astype(BF16)
 
     dg_load.wait()
     dg[...] = dg[...] + rs[...] * rs[...]
@@ -288,18 +340,19 @@
         apply(x + 2, 0)
         return total
 
-    def half_sum(d):
-        from_face(d, 0).wait_recv()
-        mine, other = vy.at[d - 2], ry.at[d - 2]
-        pout[d - 2, :, 0:rows] = block_dot(other, 0, mine, 0, half_x)
-        to_face(d, 1).start()
-        face_ref[0, 0, :, d * rows : (d + 1) * rows] = block_dot(mine, 0, other, 0, half_x)
-
-    steps = c_x // 2 - 1
-    total = lax.fori_loop(0, steps - 1, own_step, jnp.zeros((rows, rows), F32))
-    for d in (2, 3):
-        guarded(faces[d][0], lambda d=d: half_sum(d))
-    total = lax.fori_loop(steps - 1, steps, own_step, total)
+    def hand_over(d, chunk):
+        by_relay(d, 0, chunk).wait_recv()
+        by_relay(d, 1, chunk).start()
+
+    total = jnp.zeros((rows, rows), F32)
+    for step in range(c_x // 2 - 1):
+        if step < rounds - 1:
+            add_counts(step)
+            send_counts(step + 1)
+        total = lax.fori_loop(step, step + 1, own_step, total)
+        if step < 2:
+            guarded(ix == 0, lambda step=step: hand_over(0, step))
+            guarded(ix == n_x - 1, lambda step=step: hand_over(1, step))
     total = total + product(c_x - 2, 0)
     apply(c_x - 1, 1)
     own_ref[0, 0] = total + product(c_x - 1, 1)
@@ -318,20 +371,26 @@
         guarded(diagonals[d][0], corner_sum)
         guarded(jnp.logical_not(diagonals[d][0]), corner_zero)
 
-    off_ref[...] = jnp.zeros(off_ref.shape, jnp.int32)
-    for far in range(1, n_y):
-
-        def earlier(far=far):
-            to_peer(far).wait_recv()
-            off_ref[...] += cr[far, 0:1, 0:1]
-
-        guarded(iy >= far, earlier)
+    for r in range(min(c_x // 2 - 1, rounds - 1), rounds):
+        add_counts(r)
+        if r + 1 < rounds:
+            send_counts(r + 1)
+    off_ref[...] = cb_last[0:1, 0:1] - cnt[...]
 
     def finish_y(d):
-        from_face(d, 1).wait_recv()
-        face_ref[0, 0, :, d * rows : (d + 1) * rows] += pin[d - 2, :, 0:rows]
+        from_face(d, 0).wait_recv()
+        face_ref[0, 0, :, d * rows : (d + 1) * rows] = block_dot(vy.at[d - 2], 0, ry.at[d - 2], 0, c_x)
 
     def finish_x(d):
+        @pl.when(origin_of(d))
+        def _():
+            for chunk in range(2):
+                by_relay(d ^ 1, 1, chunk).wait_recv()
+
+        @pl.when(jnp.logical_not(origin_of(d)))
+        def _():
+            from_face(d, 1).wait_recv()
+
         from_face(d, 0).wait_recv()
         face_ref[0, 0, :, d * rows : (d + 1) * rows] = block_dot(vx.at[d], 0, rx.at[d], 0, c_y)
 
@@ -344,14 +403,30 @@
 
     def sent(d):
         to_face(d, 0).wait_send()
-        if d >= 2:
-            to_face(d, 1).wait_send()
+        if d < 2:
+
+            @pl.when(origin_of(d))
+            def _():
+                for chunk in range(2):
+                    by_relay(d, 0, chunk).wait_send()
+
+            @pl.when(jnp.logical_not(origin_of(d)))
+            def _():
+                to_face(d, 1).wait_send()
 
     for d in range(4):
         guarded(faces[d][0], lambda d=d: sent(d))
         guarded(diagonals[d][0], lambda d=d: to_corner(d).wait_send())
-    for far in range(1, n_y):
-        guarded(iy + far < n_y, lambda far=far: to_peer(far).wait_send())
+
+    @pl.when(is_relay)
+    def _():
+        for chunk in range(2):
+            by_relay(0, 1, chunk).wait_send()
+
+    for r in range(rounds):
+        guarded(iy + 2**r < n_y, lambda r=r: to_peer(r, 1).wait_send())
+        if r + 1 < rounds:
+            guarded(iy >= 2**r, lambda r=r: to_peer(r, 0).wait_send())
 
 
 def hand_on(*refs):
@@ -362,7 +437,7 @@
 
 def on_device(n_x, n_y, vectors, root_stiff, diag_coef, counts):
     rows, c_x, c_y, c_z = vectors.shape
-    half_x = c_x // 2
+    rounds = max(1, (n_y - 1).bit_length())
     vmem = pltpu.VMEM
     results = (
         jax.ShapeDtypeStruct((1, 1, rows, rows), F32),
@@ -386,23 +461,23 @@
             vmem((2, c_y, rows, c_z), BF16),
             vmem((c_x, rows, c_z), BF16),
             vmem((c_x, rows, c_z), BF16),
-            vmem((half_x, rows, c_z), BF16),
             vmem((c_x + 2, c_y + 2, rows, c_z), F32),
             vmem((2, c_y, rows, c_z), BF16),
             vmem((2, c_y, rows, c_z), BF16),
-            vmem((2, half_x, rows, c_z), BF16),
+            vmem((2, c_x, rows, c_z), BF16),
             vmem((2, c_y, rows, c_z), BF16),
-            vmem((2, half_x, rows, c_z), BF16),
+            vmem((2, c_x, rows, c_z), BF16),
             vmem((4, rows, c_z), BF16),
-            vmem((2, rows, c_z), F32),
-            vmem((2, rows, c_z), F32),
+            vmem((2, c_y // 4, rows, c_z), BF16),
+            vmem((rounds, 8, c_z), jnp.int32),
             vmem((8, c_z), jnp.int32),
-            vmem((n_y, 8, c_z), jnp.int32),
+            vmem((rounds, 2, 8, c_z), jnp.int32),
             pltpu.SemaphoreType.DMA((c_x + 3,)),
             pltpu.SemaphoreType.DMA((12,)),
             pltpu.SemaphoreType.DMA((12,)),
-            pltpu.SemaphoreType.DMA((n_y,)),
-            pltpu.SemaphoreType.DMA((n_y,)),
+            pltpu.SemaphoreType.DMA((rounds, 2)),
+            pltpu.SemaphoreType.DMA((rounds, 2)),
+            pltpu.SemaphoreType.DMA((2, 2, 2)),
         ],
         compiler_params=pltpu.CompilerParams(
             collective_id=0, has_side_effects=True, vmem_limit_bytes=60 * 1024 * 1024

time: 24.7 us -> 25.4 us (1.028)
  the two profiles are of different devices: /device:TPU:2 before, /device:TPU:25 now
where the time goes in v4:
time: 25.4 us; the launch traced here: 25.2 us
  Pallas kernels  23.9 us (94%)
  between operations  1.29 us (5%)
    pallas_call x1, Pallas kernels, on_device(): pl.pallas_call(functools.partial(kernel, n_x, n_y), out_shape=results, in...  21.7 us
    pallas_call x1, Pallas kernels, on_device(): pl.pallas_call(hand_on, out_shape=results, in_specs=[pl.BlockSpec(memory_...  2.19 us

profile of v4, /device:TPU:25, one launch (start us, length us, event | category | flops | bytes accessed | tf_op | source)
XLA Modules:
  0.0 25.2 jit_solution(2390575163117261766)
XLA Ops:
  1.3 21.7 %coarse.1 = (f32[1,1,64,64]{3,2,1,0:T(8,128)}, f32[1,1,64,256]{3,2,1,0:T(8,128)}, f32[1,1,64,256]{3,2,1,0:T(8,128)}, s32[1,1]{1,0:T(1,128)}) custom-call(bf16[64,8,32,128]{3,2,1,0:T(8,128)(2,1)} %vec_ref.1, f32[8,32,128]{2,1,0:T(8,128)} %rs_ref.1, f32[8,32,128]{2,1,0:T(8,128)} %dg_ref.1, s32[1,1]{1,0:T(1,128)S(6)} %copy.8.cnt_ref), custom_call_target="tpu_custom_call" | custom-call | flops 600000000 | bytes 5000000 | tf_op jit(solution)/shard_map/coarse/pallas_call | solution.py:449
  23.0 2.2 %results.1 = (f32[1,1,64,64]{3,2,1,0:T(8,128)}, f32[1,1,64,256]{3,2,1,0:T(8,128)}, f32[1,1,64,256]{3,2,1,0:T(8,128)}, s32[1,1]{1,0:T(1,128)}) custom-call(f32[1,1,64,64]{3,2,1,0:T(8,128)} %get-tuple-element.8.refs_0_, f32[1,1,64,256]{3,2,1,0:T(8,128)} %get-tuple-element.9.refs_1_, f32[1,1,64,256]{3,2,1,0:T(8,128)} %get-tuple-element.10.refs_2_, ...), custom_call_target="tpu_custom_call" | custom-call | tf_op jit(solution)/shard_map/results/pallas_call | solution.py:488

commit v5 on v4

--- a/solution.py
+++ b/solution.py
@@ -41,7 +41,6 @@
     vv,
     rs,
     dg,
-    cnt,
     wide,
     mb,
     sx,
@@ -56,7 +55,6 @@
     rc,
     rr,
     cb,
-    cb_last,
     cr,
     load_sem,
     send_sem,
@@ -66,7 +64,6 @@
     relay_sem,
 ):
     rows, c_x, c_y, c_z = vec_ref.shape
-    rounds = cb.shape[0]
     pitch = c_y + 1
     ix, iy = lax.axis_index("sx"), lax.axis_index("sy")
 
@@ -75,10 +72,8 @@
 
     rs_load = pltpu.make_async_copy(rs_ref, rs, load_sem.at[c_x])
     dg_load = pltpu.make_async_copy(dg_ref, dg, load_sem.at[c_x + 1])
-    cnt_load = pltpu.make_async_copy(cnt_ref, cnt, load_sem.at[c_x + 2])
-    cnt_load.start()
+    rs_load.start()
     load(0).start()
-    rs_load.start()
     load(c_x - 1).start()
     for x in range(1, c_x - 1):
         load(x).start()
@@ -106,6 +101,12 @@
         def _(device=device):
             pl.semaphore_signal(barrier, inc=1, device_id=device, device_id_type=MESH)
 
+    for far in range(2, n_y):
+
+        @pl.when(iy >= far)
+        def _(far=far):
+            pl.semaphore_signal(barrier, inc=1, device_id=(ix, iy - far), device_id_type=MESH)
+
     across_low, across_high = n_x // 2 - 1, n_x // 2
     is_origin = (ix == across_low) | (ix == across_high)
     is_relay = (ix == 0) | (ix == n_x - 1)
@@ -125,6 +126,7 @@
 
     greeted = sum(there.astype(jnp.int32) for there, _ in faces + diagonals)
     greeted = greeted + (is_relay | is_origin).astype(jnp.int32)
+    greeted = greeted + jnp.maximum(n_y - 2 - iy, 0)
 
     lane_r = lax.broadcasted_iota(jnp.int32, (c_z, c_z), 0)
     lane_c = lax.broadcasted_iota(jnp.int32, (c_z, c_z), 1)
@@ -141,9 +143,9 @@
         zp[x, 0] = jnp.zeros((rows, c_z), F32)
         zp[x, c_y + 1] = jnp.zeros((rows, c_z), F32)
 
-    cnt_load.wait()
-    cb[0] = jnp.broadcast_to(cnt[...], cb.shape[1:])
-    keep = lax.broadcasted_iota(jnp.int32, (rows, c_z), 0) < cnt[...]
+    count = cnt_ref[0, 0]
+    cb[...] = jnp.full(cb.shape, count, jnp.int32)
+    keep = lax.broadcasted_iota(jnp.int32, (rows, c_z), 0) < count
 
     def widen(x):
         load(x).wait()
@@ -154,24 +156,26 @@
         m = jnp.where(keep, wide[x, pl.ds(y, rows, stride=pitch), :], 0.0)
         return m, m * rs[x, y : y + 1, :]
 
-    def scale(x, side=None):
+    def smoothed(x, pieces):
+        z = jnp.dot(jnp.concatenate(pieces, axis=0), smooth, preferred_element_type=F32)
+        for y in range(c_y):
+            zp[x + 1, y + 1] = z[y * rows : (y + 1) * rows]
+
+    def scale(x):
         pieces = []
         for y in range(c_y):
             m, s = row(x, y)
-            s = s.astype(BF16)
             mb[x, y] = m.astype(BF16)
-            if side is not None:
-                sx[side, y] = s
-            pieces.append(s)
-        z = jnp.dot(jnp.concatenate(pieces, axis=0), smooth, preferred_element_type=F32)
+            pieces.append(s.astype(BF16))
+        smoothed(x, pieces)
+
+    rs_load.wait()
+    for side, x in enumerate((0, c_x - 1)):
+        widen(x)
         for y in range(c_y):
-            zp[x + 1, y + 1] = z[y * rows : (y + 1) * rows]
-
-    rs_load.wait()
-    widen(0)
-    scale(0, 0)
-    widen(c_x - 1)
-    scale(c_x - 1, 1)
+            m, s = row(x, y)
+            mb[x, y] = m.astype(BF16)
+            sx[side, y] = s.astype(BF16)
 
     def widen_step(x, _):
         widen(x)
@@ -234,14 +238,13 @@
     def from_corner(d):
         return to_corner(3 - d, d)
 
-    def to_peer(r, up):
-        far = 2**r
+    def to_peer(far):
         return pltpu.make_async_remote_copy(
-            src_ref=cb.at[r],
-            dst_ref=cr.at[r, up],
-            send_sem=csend_sem.at[r, up],
-            recv_sem=crecv_sem.at[r, up],
-            device_id=(ix, iy + far if up else iy - far),
+            src_ref=cb,
+            dst_ref=cr.at[far],
+            send_sem=csend_sem.at[far],
+            recv_sem=crecv_sem.at[far],
+            device_id=(ix, iy + far),
             device_id_type=MESH,
         )
 
@@ -259,37 +262,23 @@
             for chunk in range(2):
                 by_relay(d, 0, chunk).start()
 
+        to_face(d, 0).start()
+
         @pl.when(jnp.logical_not(origin_of(d)))
         def _():
             to_face(d, 1).start()
 
-        to_face(d, 0).start()
-
-    def send_counts(r):
-        guarded(iy + 2**r < n_y, lambda: to_peer(r, 1).start())
-        if r + 1 < rounds:
-            guarded(iy >= 2**r, lambda: to_peer(r, 0).start())
-
-    def add_counts(r):
-        far = 2**r
-        cb_next = cb.at[r + 1] if r + 1 < rounds else cb_last
-        cb_next[...] = cb[r]
-
-        @pl.when(iy >= far)
-        def _():
-            to_peer(r, 1).wait_recv()
-            cb_next[...] += cr[r, 1]
-
-        if r + 1 < rounds:
-            guarded(iy + far < n_y, lambda: to_peer(r, 0).wait_recv())
-
-    send_counts(0)
+    for far in range(1, n_y):
+        guarded(iy + far < n_y, lambda far=far: to_peer(far).start())
     for d in (1, 0):
         guarded(faces[d][0], lambda d=d: send_x(d))
     for d in (3, 2):
         guarded(faces[d][0], lambda d=d: to_face(d, 0).start())
     for d in range(4):
         guarded(diagonals[d][0], lambda d=d: to_corner(d).start())
+
+    for side, x in enumerate((0, c_x - 1)):
+        smoothed(x, [sx[side, y] for y in range(c_y)])
 
     def scale_step(x, _):
         scale(x)
@@ -346,9 +335,6 @@
 
     total = jnp.zeros((rows, rows), F32)
     for step in range(c_x // 2 - 1):
-        if step < rounds - 1:
-            add_counts(step)
-            send_counts(step + 1)
         total = lax.fori_loop(step, step + 1, own_step, total)
         if step < 2:
             guarded(ix == 0, lambda step=step: hand_over(0, step))
@@ -371,17 +357,26 @@
         guarded(diagonals[d][0], corner_sum)
         guarded(jnp.logical_not(diagonals[d][0]), corner_zero)
 
-    for r in range(min(c_x // 2 - 1, rounds - 1), rounds):
-        add_counts(r)
-        if r + 1 < rounds:
-            send_counts(r + 1)
-    off_ref[...] = cb_last[0:1, 0:1] - cnt[...]
+    off_ref[...] = jnp.zeros(off_ref.shape, jnp.int32)
+    for far in range(1, n_y):
+
+        def earlier(far=far):
+            to_peer(far).wait_recv()
+            off_ref[...] += cr[far, 0:1, 0:1]
+
+        guarded(iy >= far, earlier)
 
     def finish_y(d):
         from_face(d, 0).wait_recv()
         face_ref[0, 0, :, d * rows : (d + 1) * rows] = block_dot(vy.at[d - 2], 0, ry.at[d - 2], 0, c_x)
 
-    def finish_x(d):
+    half = c_y // 2
+
+    def first_x(d):
+        from_face(d, 0).wait_recv()
+        face_ref[0, 0, :, d * rows : (d + 1) * rows] = block_dot(vx.at[d], 0, rx.at[d], 0, half)
+
+    def last_x(d):
         @pl.when(origin_of(d))
         def _():
             for chunk in range(2):
@@ -391,15 +386,19 @@
         def _():
             from_face(d, 1).wait_recv()
 
-        from_face(d, 0).wait_recv()
-        face_ref[0, 0, :, d * rows : (d + 1) * rows] = block_dot(vx.at[d], 0, rx.at[d], 0, c_y)
+        face_ref[0, 0, :, d * rows : (d + 1) * rows] += block_dot(vx.at[d], half, rx.at[d], half, half)
 
     def face_zero(d):
         face_ref[0, 0, :, d * rows : (d + 1) * rows] = jnp.zeros((rows, rows), F32)
 
-    for d in (2, 3, 0, 1):
-        guarded(faces[d][0], lambda d=d: (finish_x if d < 2 else finish_y)(d))
+    for d in range(4):
         guarded(jnp.logical_not(faces[d][0]), lambda d=d: face_zero(d))
+    for d in (2, 3):
+        guarded(faces[d][0], lambda d=d: finish_y(d))
+    for d in (0, 1):
+        guarded(faces[d][0], lambda d=d: first_x(d))
+    for d in (0, 1):
+        guarded(faces[d][0], lambda d=d: last_x(d))
 
     def sent(d):
         to_face(d, 0).wait_send()
@@ -423,21 +422,22 @@
         for chunk in range(2):
             by_relay(0, 1, chunk).wait_send()
 
-    for r in range(rounds):
-        guarded(iy + 2**r < n_y, lambda r=r: to_peer(r, 1).wait_send())
-        if r + 1 < rounds:
-            guarded(iy >= 2**r, lambda r=r: to_peer(r, 0).wait_send())
-
-
-def hand_on(*refs):
-    n = len(refs) // 2
-    for i in range(n):
-        refs[n + i][...] = refs[i][...]
+    for far in range(1, n_y):
+        guarded(iy + far < n_y, lambda far=far: to_peer(far).wait_send())
+
+
+def hand_on(own_in, face_in, corner_in, off_in, own_out, face_out, corner_out, off_out, sems):
+    pairs = [(own_in, own_out), (face_in, face_out), (corner_in, corner_out)]
+    copies = [pltpu.make_async_copy(a, b, sems.at[i]) for i, (a, b) in enumerate(pairs)]
+    for copy in copies:
+        copy.start()
+    off_out[...] = off_in[...]
+    for copy in copies:
+        copy.wait()
 
 
 def on_device(n_x, n_y, vectors, root_stiff, diag_coef, counts):
     rows, c_x, c_y, c_z = vectors.shape
-    rounds = max(1, (n_y - 1).bit_length())
     vmem = pltpu.VMEM
     results = (
         jax.ShapeDtypeStruct((1, 1, rows, rows), F32),
@@ -449,13 +449,12 @@
     outputs = pl.pallas_call(
         functools.partial(kernel, n_x, n_y),
         out_shape=results,
-        in_specs=[anywhere] * 3 + [pl.BlockSpec(memory_space=pltpu.HBM)],
+        in_specs=[anywhere] * 3 + [pl.BlockSpec(memory_space=pltpu.SMEM)],
         out_specs=[pl.BlockSpec(memory_space=vmem)] * 4,
         scratch_shapes=[
             vmem((c_x, rows, c_y, c_z), BF16),
             vmem((c_x, c_y, c_z), F32),
             vmem((c_x, c_y, c_z), F32),
-            vmem((1, 1), jnp.int32),
             vmem((c_x, rows * (c_y + 1) + 7, c_z), F32),
             vmem((c_x, c_y, rows, c_z), BF16),
             vmem((2, c_y, rows, c_z), BF16),
@@ -469,18 +468,17 @@
             vmem((2, c_x, rows, c_z), BF16),
             vmem((4, rows, c_z), BF16),
             vmem((2, c_y // 4, rows, c_z), BF16),
-            vmem((rounds, 8, c_z), jnp.int32),
             vmem((8, c_z), jnp.int32),
-            vmem((rounds, 2, 8, c_z), jnp.int32),
-            pltpu.SemaphoreType.DMA((c_x + 3,)),
+            vmem((n_y, 8, c_z), jnp.int32),
+            pltpu.SemaphoreType.DMA((c_x + 2,)),
             pltpu.SemaphoreType.DMA((12,)),
             pltpu.SemaphoreType.DMA((12,)),
-            pltpu.SemaphoreType.DMA((rounds, 2)),
-            pltpu.SemaphoreType.DMA((rounds, 2)),
+            pltpu.SemaphoreType.DMA((n_y,)),
+            pltpu.SemaphoreType.DMA((n_y,)),
             pltpu.SemaphoreType.DMA((2, 2, 2)),
         ],
         compiler_params=pltpu.CompilerParams(
-            collective_id=0, has_side_effects=True, vmem_limit_bytes=60 * 1024 * 1024
+            collective_id=0, has_side_effects=True, vmem_limit_bytes=55040 * 1024
         ),
         cost_estimate=pl.CostEstimate(flops=600_000_000, bytes_accessed=5_000_000, transcendentals=0),
         name="coarse",
@@ -488,9 +486,11 @@
     return pl.pallas_call(
         hand_on,
         out_shape=results,
-        in_specs=[pl.BlockSpec(memory_space=vmem)] * len(results),
-        out_specs=[pl.BlockSpec(memory_space=vmem)] * len(results),
+        in_specs=[anywhere] * 3 + [pl.BlockSpec(memory_space=vmem)],
+        out_specs=[anywhere] * 3 + [pl.BlockSpec(memory_space=vmem)],
+        scratch_shapes=[pltpu.SemaphoreType.DMA((3,))],
         name="results",
+        compiler_params=pltpu.CompilerParams(vmem_limit_bytes=4 * 1024 * 1024),
     )(*outputs)
 
 

time: 25.4 us -> 21.7 us (0.85)
  the two profiles are of different devices: /device:TPU:25 before, /device:TPU:31 now
where the time goes in v5:
time: 21.7 us; the launch traced here: 21.6 us
  Pallas kernels  20.3 us (94%)
  between operations  1.29 us (6%)
    pallas_call x1, Pallas kernels, on_device(): pl.pallas_call(functools.partial(kernel, n_x, n_y), out_shape=results, in...  18.5 us
    pallas_call x1, Pallas kernels, on_device(): pl.pallas_call(hand_on, out_shape=results, in_specs=[anywhere] * 3 + [pl....  1.76 us

profile of v5, /device:TPU:31, one launch (start us, length us, event | category | flops | bytes accessed | tf_op | source)
XLA Modules:
  0.0 21.6 jit_solution(5599840874375345087)
XLA Ops:
  1.3 18.5 %coarse.1 = (f32[1,1,64,64]{3,2,1,0:T(8,128)S(1)}, f32[1,1,64,256]{3,2,1,0:T(8,128)S(1)}, f32[1,1,64,256]{3,2,1,0:T(8,128)S(1)}, s32[1,1]{1,0:T(1,128)}) custom-call(bf16[64,8,32,128]{3,2,1,0:T(8,128)(2,1)} %vec_ref.1, f32[8,32,128]{2,1,0:T(8,128)} %rs_ref.1, f32[8,32,128]{2,1,0:T(8,128)} %dg_ref.1, s32[1,1]{1,0:T(1,128)S(6)} %copy.8.cnt_ref), custom_call_target="tpu_custom_call" | custom-call | flops 600000000 | bytes 5000000 | tf_op jit(solution)/shard_map/coarse/pallas_call | solution.py:449
  19.8 1.8 %results.1 = (f32[1,1,64,64]{3,2,1,0:T(8,128)}, f32[1,1,64,256]{3,2,1,0:T(8,128)}, f32[1,1,64,256]{3,2,1,0:T(8,128)}, s32[1,1]{1,0:T(1,128)}) custom-call(f32[1,1,64,64]{3,2,1,0:T(8,128)S(1)} %get-tuple-element.8.own_in, f32[1,1,64,256]{3,2,1,0:T(8,128)S(1)} %get-tuple-element.9.face_in, f32[1,1,64,256]{3,2,1,0:T(8,128)S(1)} %get-tuple-element.10.corner_in, ...), custom_call_target="tpu_custom_call" | custom-call | tf_op jit(solution)/shard_map/results/pallas_call | solution.py:486

commit v6 on v5

--- a/solution.py
+++ b/solution.py
@@ -54,6 +54,7 @@
     ry,
     rc,
     rr,
+    vc,
     cb,
     cr,
     load_sem,
@@ -67,17 +68,10 @@
     pitch = c_y + 1
     ix, iy = lax.axis_index("sx"), lax.axis_index("sy")
 
-    def load(x):
-        return pltpu.make_async_copy(vec_ref.at[:, x], vv.at[x], load_sem.at[x])
-
-    rs_load = pltpu.make_async_copy(rs_ref, rs, load_sem.at[c_x])
-    dg_load = pltpu.make_async_copy(dg_ref, dg, load_sem.at[c_x + 1])
-    rs_load.start()
-    load(0).start()
-    load(c_x - 1).start()
-    for x in range(1, c_x - 1):
-        load(x).start()
-    dg_load.start()
+    def guarded(there, action):
+        @pl.when(there)
+        def _():
+            action()
 
     low_x, high_x = ix > 0, ix < n_x - 1
     low_y, high_y = iy > 0, iy < n_y - 1
@@ -124,9 +118,36 @@
     def _():
         pl.semaphore_signal(barrier, inc=1, device_id=target_from, device_id_type=MESH)
 
+    def load(x):
+        return pltpu.make_async_copy(vec_ref.at[:, x], vv.at[x], load_sem.at[x])
+
+    rs_load = pltpu.make_async_copy(rs_ref, rs, load_sem.at[c_x])
+    dg_load = pltpu.make_async_copy(dg_ref, dg, load_sem.at[c_x + 1])
+    rs_load.start()
+    load(0).start()
+    load(c_x - 1).start()
+    for x in range(1, c_x - 1):
+        load(x).start()
+    dg_load.start()
+
     greeted = sum(there.astype(jnp.int32) for there, _ in faces + diagonals)
     greeted = greeted + (is_relay | is_origin).astype(jnp.int32)
     greeted = greeted + jnp.maximum(n_y - 2 - iy, 0)
+
+    def zero_layers(ref):
+        def step(i, _):
+            ref[i] = jnp.zeros((rows, c_z), BF16)
+            return _
+
+        lax.fori_loop(0, ref.shape[0], step, 0)
+
+    for d in range(4):
+        layers = rx.at[d] if d < 2 else ry.at[d - 2]
+        guarded(jnp.logical_not(faces[d][0]), lambda layers=layers: zero_layers(layers))
+
+        @pl.when(jnp.logical_not(diagonals[d][0]))
+        def _(d=d):
+            rc[d] = jnp.zeros((rows, c_z), BF16)
 
     lane_r = lax.broadcasted_iota(jnp.int32, (c_z, c_z), 0)
     lane_c = lax.broadcasted_iota(jnp.int32, (c_z, c_z), 1)
@@ -248,11 +269,6 @@
             device_id_type=MESH,
         )
 
-    def guarded(there, action):
-        @pl.when(there)
-        def _():
-            action()
-
     def origin_of(d):
         return ix == (across_high, across_low)[d]
 
@@ -268,14 +284,14 @@
         def _():
             to_face(d, 1).start()
 
-    for far in range(1, n_y):
-        guarded(iy + far < n_y, lambda far=far: to_peer(far).start())
+    for d in range(4):
+        guarded(diagonals[d][0], lambda d=d: to_corner(d).start())
     for d in (1, 0):
         guarded(faces[d][0], lambda d=d: send_x(d))
     for d in (3, 2):
         guarded(faces[d][0], lambda d=d: to_face(d, 0).start())
-    for d in range(4):
-        guarded(diagonals[d][0], lambda d=d: to_corner(d).start())
+    for far in range(1, n_y):
+        guarded(iy + far < n_y, lambda far=far: to_peer(far).start())
 
     for side, x in enumerate((0, c_x - 1)):
         smoothed(x, [sx[side, y] for y in range(c_y)])
@@ -344,18 +360,8 @@
     own_ref[0, 0] = total + product(c_x - 1, 1)
 
     for d in range(4):
-
-        def corner_sum(d=d):
-            from_corner(d).wait_recv()
-            x, y = (0, c_x - 1)[d // 2], (0, c_y - 1)[d % 2]
-            mine = (-0.25 * zp[x + 1, y + 1]).astype(BF16)
-            corner_ref[0, 0, :, d * rows : (d + 1) * rows] = row_dot(mine, rc[d])
-
-        def corner_zero(d=d):
-            corner_ref[0, 0, :, d * rows : (d + 1) * rows] = jnp.zeros((rows, rows), F32)
-
-        guarded(diagonals[d][0], corner_sum)
-        guarded(jnp.logical_not(diagonals[d][0]), corner_zero)
+        x, y = (0, c_x - 1)[d // 2], (0, c_y - 1)[d % 2]
+        vc[d] = (-0.25 * zp[x + 1, y + 1]).astype(BF16)
 
     off_ref[...] = jnp.zeros(off_ref.shape, jnp.int32)
     for far in range(1, n_y):
@@ -366,17 +372,9 @@
 
         guarded(iy >= far, earlier)
 
-    def finish_y(d):
+    def arrived_x(d):
         from_face(d, 0).wait_recv()
-        face_ref[0, 0, :, d * rows : (d + 1) * rows] = block_dot(vy.at[d - 2], 0, ry.at[d - 2], 0, c_x)
-
-    half = c_y // 2
-
-    def first_x(d):
-        from_face(d, 0).wait_recv()
-        face_ref[0, 0, :, d * rows : (d + 1) * rows] = block_dot(vx.at[d], 0, rx.at[d], 0, half)
-
-    def last_x(d):
+
         @pl.when(origin_of(d))
         def _():
             for chunk in range(2):
@@ -386,19 +384,16 @@
         def _():
             from_face(d, 1).wait_recv()
 
-        face_ref[0, 0, :, d * rows : (d + 1) * rows] += block_dot(vx.at[d], half, rx.at[d], half, half)
-
-    def face_zero(d):
-        face_ref[0, 0, :, d * rows : (d + 1) * rows] = jnp.zeros((rows, rows), F32)
-
     for d in range(4):
-        guarded(jnp.logical_not(faces[d][0]), lambda d=d: face_zero(d))
+        guarded(diagonals[d][0], lambda d=d: from_corner(d).wait_recv())
     for d in (2, 3):
-        guarded(faces[d][0], lambda d=d: finish_y(d))
+        guarded(faces[d][0], lambda d=d: from_face(d, 0).wait_recv())
     for d in (0, 1):
-        guarded(faces[d][0], lambda d=d: first_x(d))
-    for d in (0, 1):
-        guarded(faces[d][0], lambda d=d: last_x(d))
+        guarded(faces[d][0], lambda d=d: arrived_x(d))
+    products = [block_dot(vx.at[d], 0, rx.at[d], 0, c_y) for d in range(2)]
+    products += [block_dot(vy.at[d], 0, ry.at[d], 0, c_x) for d in range(2)]
+    face_ref[0, 0] = along_lanes(products)
+    corner_ref[0, 0] = along_lanes([row_dot(vc[d], rc[d]) for d in range(4)])
 
     def sent(d):
         to_face(d, 0).wait_send()
@@ -468,6 +463,7 @@
             vmem((2, c_x, rows, c_z), BF16),
             vmem((4, rows, c_z), BF16),
             vmem((2, c_y // 4, rows, c_z), BF16),
+            vmem((4, rows, c_z), BF16),
             vmem((8, c_z), jnp.int32),
             vmem((n_y, 8, c_z), jnp.int32),
             pltpu.SemaphoreType.DMA((c_x + 2,)),

time: 21.7 us -> 20.5 us (0.945)
  the two profiles are of different devices: /device:TPU:31 before, /device:TPU:25 now
where the time goes in v6:
time: 20.5 us; the launch traced here: 20.1 us
  Pallas kernels  18.8 us (92%)
  between operations  1.29 us (6%)
    pallas_call x1, Pallas kernels, on_device(): pl.pallas_call(functools.partial(kernel, n_x, n_y), out_shape=results, in...  17.1 us
    pallas_call x1, Pallas kernels, on_device(): pl.pallas_call(hand_on, out_shape=results, in_specs=[anywhere] * 3 + [pl....  1.76 us

profile of v6, /device:TPU:25, one launch (start us, length us, event | category | flops | bytes accessed | tf_op | source)
XLA Modules:
  0.0 20.1 jit_solution(3275623034035232227)
XLA Ops:
  1.3 17.1 %coarse.1 = (f32[1,1,64,64]{3,2,1,0:T(8,128)S(1)}, f32[1,1,64,256]{3,2,1,0:T(8,128)S(1)}, f32[1,1,64,256]{3,2,1,0:T(8,128)S(1)}, s32[1,1]{1,0:T(1,128)}) custom-call(bf16[64,8,32,128]{3,2,1,0:T(8,128)(2,1)} %vec_ref.1, f32[8,32,128]{2,1,0:T(8,128)} %rs_ref.1, f32[8,32,128]{2,1,0:T(8,128)} %dg_ref.1, s32[1,1]{1,0:T(1,128)S(6)} %copy.8.cnt_ref), custom_call_target="tpu_custom_call" | custom-call | flops 600000000 | bytes 5000000 | tf_op jit(solution)/shard_map/coarse/pallas_call | solution.py:444
  18.3 1.8 %results.1 = (f32[1,1,64,64]{3,2,1,0:T(8,128)}, f32[1,1,64,256]{3,2,1,0:T(8,128)}, f32[1,1,64,256]{3,2,1,0:T(8,128)}, s32[1,1]{1,0:T(1,128)}) custom-call(f32[1,1,64,64]{3,2,1,0:T(8,128)S(1)} %get-tuple-element.8.own_in, f32[1,1,64,256]{3,2,1,0:T(8,128)S(1)} %get-tuple-element.9.face_in, f32[1,1,64,256]{3,2,1,0:T(8,128)S(1)} %get-tuple-element.10.corner_in, ...), custom_call_target="tpu_custom_call" | custom-call | tf_op jit(solution)/shard_map/results/pallas_call | solution.py:482

commit v7 on v6

--- a/solution.py
+++ b/solution.py
@@ -368,13 +368,11 @@
 
         def earlier(far=far):
             to_peer(far).wait_recv()
-            off_ref[...] += cr[far, 0:1, 0:1]
+            off_ref[...] += cr[far]
 
         guarded(iy >= far, earlier)
 
-    def arrived_x(d):
-        from_face(d, 0).wait_recv()
-
+    def rest_x(d):
         @pl.when(origin_of(d))
         def _():
             for chunk in range(2):
@@ -384,16 +382,22 @@
         def _():
             from_face(d, 1).wait_recv()
 
+    half = c_y // 2
     for d in range(4):
         guarded(diagonals[d][0], lambda d=d: from_corner(d).wait_recv())
+    for d in (0, 1):
+        guarded(faces[d][0], lambda d=d: from_face(d, 0).wait_recv())
+    corner_ref[0, 0] = along_lanes([row_dot(vc[d], rc[d]) for d in range(4)])
+    products = [block_dot(vx.at[d], 0, rx.at[d], 0, half) for d in range(2)]
+    face_ref[0, 0, :, 0 : 2 * rows] = along_lanes(products)
     for d in (2, 3):
         guarded(faces[d][0], lambda d=d: from_face(d, 0).wait_recv())
     for d in (0, 1):
-        guarded(faces[d][0], lambda d=d: arrived_x(d))
-    products = [block_dot(vx.at[d], 0, rx.at[d], 0, c_y) for d in range(2)]
-    products += [block_dot(vy.at[d], 0, ry.at[d], 0, c_x) for d in range(2)]
-    face_ref[0, 0] = along_lanes(products)
-    corner_ref[0, 0] = along_lanes([row_dot(vc[d], rc[d]) for d in range(4)])
+        guarded(faces[d][0], lambda d=d: rest_x(d))
+    products = [block_dot(vx.at[d], half, rx.at[d], half, half) for d in range(2)]
+    face_ref[0, 0, :, 0 : 2 * rows] += along_lanes(products)
+    products = [block_dot(vy.at[d], 0, ry.at[d], 0, c_x) for d in range(2)]
+    face_ref[0, 0, :, 2 * rows : 4 * rows] = along_lanes(products)
 
     def sent(d):
         to_face(d, 0).wait_send()
@@ -421,14 +425,18 @@
         guarded(iy + far < n_y, lambda far=far: to_peer(far).wait_send())
 
 
-def hand_on(own_in, face_in, corner_in, off_in, own_out, face_out, corner_out, off_out, sems):
-    pairs = [(own_in, own_out), (face_in, face_out), (corner_in, corner_out)]
+def hand_on(own_in, face_in, corner_in, off_in, own_out, face_out, corner_out, off_out, wide, first, sems):
+    pairs = [(off_in, wide), (face_in, face_out), (corner_in, corner_out), (own_in, own_out)]
     copies = [pltpu.make_async_copy(a, b, sems.at[i]) for i, (a, b) in enumerate(pairs)]
     for copy in copies:
         copy.start()
-    off_out[...] = off_in[...]
-    for copy in copies:
+    copies[0].wait()
+    first[...] = wide[0:1, 0:1]
+    last = pltpu.make_async_copy(first, off_out, sems.at[len(pairs)])
+    last.start()
+    for copy in copies[1:]:
         copy.wait()
+    last.wait()
 
 
 def on_device(n_x, n_y, vectors, root_stiff, diag_coef, counts):
@@ -443,7 +451,7 @@
     anywhere = pl.BlockSpec(memory_space=pl.ANY)
     outputs = pl.pallas_call(
         functools.partial(kernel, n_x, n_y),
-        out_shape=results,
+        out_shape=results[:3] + (jax.ShapeDtypeStruct((8, c_z), jnp.int32),),
         in_specs=[anywhere] * 3 + [pl.BlockSpec(memory_space=pltpu.SMEM)],
         out_specs=[pl.BlockSpec(memory_space=vmem)] * 4,
         scratch_shapes=[
@@ -482,9 +490,13 @@
     return pl.pallas_call(
         hand_on,
         out_shape=results,
-        in_specs=[anywhere] * 3 + [pl.BlockSpec(memory_space=vmem)],
-        out_specs=[anywhere] * 3 + [pl.BlockSpec(memory_space=vmem)],
-        scratch_shapes=[pltpu.SemaphoreType.DMA((3,))],
+        in_specs=[anywhere] * 4,
+        out_specs=[anywhere] * 4,
+        scratch_shapes=[
+            vmem((8, c_z), jnp.int32),
+            vmem((1, 1), jnp.int32),
+            pltpu.SemaphoreType.DMA((5,)),
+        ],
         name="results",
         compiler_params=pltpu.CompilerParams(vmem_limit_bytes=4 * 1024 * 1024),
     )(*outputs)

time: 20.5 us -> 18.6 us (0.907); the launches traced: 20.1 us -> 18.4 us
  Pallas kernels: 18.8 us -> 17.2 us
    pallas_call x2, Pallas kernels: 18.8 us -> 17.2 us  [the longest x1 16.4 us: on_device(): pl.pallas_call(functools.partial(kernel, n_x, n_y), out_shape=results[:3]...]
where the time goes in v7:
time: 18.6 us; the launch traced here: 18.4 us
  Pallas kernels  17.2 us (92%)
  between operations  1.29 us (7%)
    pallas_call x1, Pallas kernels, on_device(): pl.pallas_call(functools.partial(kernel, n_x, n_y), out_shape=results[:3]...  16.4 us
    pallas_call x1, Pallas kernels, on_device(): pl.pallas_call(hand_on, out_shape=results, in_specs=[anywhere] * 4, out_s...  0.71 us

profile of v7, /device:TPU:25, one launch (start us, length us, event | category | flops | bytes accessed | tf_op | source)
XLA Modules:
  0.0 18.4 jit_solution(10218929050751378593)
XLA Ops:
  1.3 16.4 %coarse.1 = (f32[1,1,64,64]{3,2,1,0:T(8,128)S(1)}, f32[1,1,64,256]{3,2,1,0:T(8,128)S(1)}, f32[1,1,64,256]{3,2,1,0:T(8,128)S(1)}, s32[8,128]{1,0:T(8,128)S(1)}) custom-call(bf16[64,8,32,128]{3,2,1,0:T(8,128)(2,1)} %vec_ref.1, f32[8,32,128]{2,1,0:T(8,128)} %rs_ref.1, f32[8,32,128]{2,1,0:T(8,128)} %dg_ref.1, s32[1,1]{1,0:T(1,128)S(6)} %copy.8.cnt_ref), custom_call_target="tpu_custom_call" | custom-call | flops 600000000 | bytes 5000000 | tf_op jit(solution)/shard_map/coarse/pallas_call | solution.py:452
  17.7 0.7 %results.1 = (f32[1,1,64,64]{3,2,1,0:T(8,128)}, f32[1,1,64,256]{3,2,1,0:T(8,128)}, f32[1,1,64,256]{3,2,1,0:T(8,128)}, s32[1,1]{1,0:T(1,128)}) custom-call(f32[1,1,64,64]{3,2,1,0:T(8,128)S(1)} %get-tuple-element.8.own_in, f32[1,1,64,256]{3,2,1,0:T(8,128)S(1)} %get-tuple-element.9.face_in, f32[1,1,64,256]{3,2,1,0:T(8,128)S(1)} %get-tuple-element.10.corner_in, ...), custom_call_target="tpu_custom_call" | custom-call | tf_op jit(solution)/shard_map/results/pallas_call | solution.py:490

commit v8 on v7

--- a/solution.py
+++ b/solution.py
@@ -10,6 +10,7 @@
 MESH = pl.DeviceIdType.MESH
 F32 = jnp.float32
 BF16 = jnp.bfloat16
+SHARE = 16
 
 
 def row_dot(left, right):
@@ -44,8 +45,7 @@
     wide,
     mb,
     sx,
-    sy0,
-    sy1,
+    sy,
     zp,
     ab,
     vx,
@@ -63,8 +63,11 @@
     csend_sem,
     crecv_sem,
     relay_sem,
+    across_sem,
 ):
     rows, c_x, c_y, c_z = vec_ref.shape
+    direct = c_y * SHARE // 32
+    chunk_rows = (c_y - direct) // 2
     pitch = c_y + 1
     ix, iy = lax.axis_index("sx"), lax.axis_index("sy")
 
@@ -81,15 +84,22 @@
         (low_y, (ix, iy - 1)),
         (high_y, (ix, iy + 1)),
     ]
-    diagonals = [
-        (low_x & low_y, (ix - 1, iy - 1)),
-        (low_x & high_y, (ix - 1, iy + 1)),
-        (high_x & low_y, (ix + 1, iy - 1)),
-        (high_x & high_y, (ix + 1, iy + 1)),
-    ]
+    across_low, across_high = n_x // 2 - 1, n_x // 2
+
+    def at_once(d):
+        return (ix == (across_high, across_low)[d]) | (ix == (n_x - 2, n_x - 3)[d])
+
+    def place(x):
+        return (0, *range(2, c_x), 1)[x]
+
+    def origin_of(d):
+        return ix == (across_high, across_low)[d]
+
+    def across(d, side):
+        return faces[d][1][0], iy - 1 + 2 * side
 
     barrier = pltpu.get_barrier_semaphore()
-    for there, device in faces + diagonals:
+    for there, device in faces:
 
         @pl.when(there)
         def _(device=device):
@@ -101,7 +111,6 @@
         def _(far=far):
             pl.semaphore_signal(barrier, inc=1, device_id=(ix, iy - far), device_id_type=MESH)
 
-    across_low, across_high = n_x // 2 - 1, n_x // 2
     is_origin = (ix == across_low) | (ix == across_high)
     is_relay = (ix == 0) | (ix == n_x - 1)
     via_y = iy + 1 - 2 * lax.rem(iy, 2)
@@ -130,8 +139,16 @@
         load(x).start()
     dg_load.start()
 
-    greeted = sum(there.astype(jnp.int32) for there, _ in faces + diagonals)
+    greeted = sum(there.astype(jnp.int32) for there, _ in faces)
     greeted = greeted + (is_relay | is_origin).astype(jnp.int32)
+    for side, there in enumerate((low_y, high_y)):
+        for d in range(2):
+
+            @pl.when(at_once(d) & there)
+            def _(side=side, d=d):
+                pl.semaphore_signal(barrier, inc=1, device_id=across(d, side), device_id_type=MESH)
+
+        greeted = greeted + ((at_once(0) | at_once(1)) & there).astype(jnp.int32)
     greeted = greeted + jnp.maximum(n_y - 2 - iy, 0)
 
     def zero_layers(ref):
@@ -145,9 +162,18 @@
         layers = rx.at[d] if d < 2 else ry.at[d - 2]
         guarded(jnp.logical_not(faces[d][0]), lambda layers=layers: zero_layers(layers))
 
-        @pl.when(jnp.logical_not(diagonals[d][0]))
-        def _(d=d):
-            rc[d] = jnp.zeros((rows, c_z), BF16)
+        if d < 2:
+
+            @pl.when(jnp.logical_not(faces[d][0]))
+            def _(d=d):
+                rc[2 * d] = jnp.zeros((rows, c_z), BF16)
+                rc[2 * d + 1] = jnp.zeros((rows, c_z), BF16)
+
+            for side, there in enumerate((low_y, high_y)):
+
+                @pl.when(at_once(d) & jnp.logical_not(there))
+                def _(d=d, side=side):
+                    rc[2 * d + side] = jnp.zeros((rows, c_z), BF16)
 
     lane_r = lax.broadcasted_iota(jnp.int32, (c_z, c_z), 0)
     lane_c = lax.broadcasted_iota(jnp.int32, (c_z, c_z), 1)
@@ -204,23 +230,24 @@
 
     lax.fori_loop(1, c_x - 1, widen_step, 0)
     for x in range(c_x):
-        sy0[x] = row(x, 0)[1].astype(BF16)
-        sy1[x] = row(x, c_y - 1)[1].astype(BF16)
+        sy[0, place(x)] = row(x, 0)[1].astype(BF16)
+        sy[1, place(x)] = row(x, c_y - 1)[1].astype(BF16)
 
     pl.semaphore_wait(barrier, greeted)
 
     def to_face(d, part, to=None):
         opposite = d ^ 1
         if d < 2:
-            piece = pl.ds(part * (c_y // 2), c_y // 2)
+            piece = pl.ds(direct, c_y - direct) if part else pl.ds(0, direct)
             src, dst = sx.at[d, piece], rx.at[opposite, piece]
         else:
-            src, dst = (sy0, sy1)[d - 2], ry.at[opposite - 2]
+            piece = pl.ds(2, c_x - 2) if part else pl.ds(0, 2)
+            src, dst = sy.at[d - 2, piece], ry.at[opposite - 2, piece]
         return pltpu.make_async_remote_copy(
             src_ref=src,
             dst_ref=dst,
-            send_sem=send_sem.at[part * 2 + d if d < 2 else 2 + d],
-            recv_sem=recv_sem.at[part * 2 + opposite if d < 2 else 2 + opposite],
+            send_sem=send_sem.at[part * 4 + d],
+            recv_sem=recv_sem.at[part * 4 + opposite],
             device_id=faces[d if to is None else to][1],
             device_id_type=MESH,
         )
@@ -230,7 +257,7 @@
 
     def by_relay(d, leg, chunk):
         opposite = d ^ 1
-        piece = pl.ds(c_y // 2 + chunk * (c_y // 4), c_y // 4)
+        piece = pl.ds(direct + chunk * chunk_rows, chunk_rows)
         src, dst = [
             (sx.at[d, piece], rr.at[chunk]),
             (rr.at[chunk], rx.at[opposite, piece]),
@@ -245,19 +272,36 @@
         )
 
     def to_corner(d, to=None):
-        opposite = 3 - d
-        side = (sy0, sy1)[d % 2]
+        opposite = d ^ 1
         return pltpu.make_async_remote_copy(
-            src_ref=side.at[(0, c_x - 1)[d // 2]],
-            dst_ref=rc.at[opposite],
+            src_ref=ry.at[pl.ds(0, 2), d],
+            dst_ref=rc.at[pl.ds(2 * opposite, 2)],
             send_sem=send_sem.at[8 + d],
             recv_sem=recv_sem.at[8 + opposite],
-            device_id=diagonals[d if to is None else to][1],
+            device_id=faces[d if to is None else to][1],
             device_id_type=MESH,
         )
 
+    def to_across(d, side, device=None):
+        return pltpu.make_async_remote_copy(
+            src_ref=sy.at[side, d],
+            dst_ref=rc.at[2 * (d ^ 1) + 1 - side],
+            send_sem=across_sem.at[0, side],
+            recv_sem=across_sem.at[1, 1 - side],
+            device_id=across(d, side) if device is None else device,
+            device_id_type=MESH,
+        )
+
+    def from_across(d, side):
+        return to_across(d ^ 1, 1 - side, across(d, side))
+
+    def at_across(action):
+        for side, there in enumerate((low_y, high_y)):
+            for d in range(2):
+                guarded(at_once(d) & there, lambda side=side, d=d: action(d, side))
+
     def from_corner(d):
-        return to_corner(3 - d, d)
+        return to_corner(d ^ 1, d)
 
     def to_peer(far):
         return pltpu.make_async_remote_copy(
@@ -269,8 +313,8 @@
             device_id_type=MESH,
         )
 
-    def origin_of(d):
-        return ix == (across_high, across_low)[d]
+    def onward(d):
+        return faces[d][0] & jnp.logical_not(at_once(d))
 
     def send_x(d):
         @pl.when(origin_of(d))
@@ -284,12 +328,13 @@
         def _():
             to_face(d, 1).start()
 
-    for d in range(4):
-        guarded(diagonals[d][0], lambda d=d: to_corner(d).start())
+    for d in (3, 2):
+        guarded(faces[d][0], lambda d=d: to_face(d, 0).start())
+    at_across(lambda d, side: to_across(d, side).start())
     for d in (1, 0):
         guarded(faces[d][0], lambda d=d: send_x(d))
     for d in (3, 2):
-        guarded(faces[d][0], lambda d=d: to_face(d, 0).start())
+        guarded(faces[d][0], lambda d=d: to_face(d, 1).start())
     for far in range(1, n_y):
         guarded(iy + far < n_y, lambda far=far: to_peer(far).start())
 
@@ -309,7 +354,7 @@
             ).astype(BF16)
     for side, y in enumerate((1, c_y)):
         for x in range(c_x):
-            vy[side, x] = (
+            vy[side, place(x)] = (
                 -0.25 * ((zp[x, y] + zp[x + 2, y]) + 2.0 * zp[x + 1, y])
             ).astype(BF16)
 
@@ -345,6 +390,12 @@
         apply(x + 2, 0)
         return total
 
+    def hand_on_corners():
+        for d in (2, 3):
+            guarded(faces[d][0], lambda d=d: from_face(d, 0).wait_recv())
+        for d in (0, 1):
+            guarded(onward(d), lambda d=d: to_corner(d).start())
+
     def hand_over(d, chunk):
         by_relay(d, 0, chunk).wait_recv()
         by_relay(d, 1, chunk).start()
@@ -355,6 +406,8 @@
         if step < 2:
             guarded(ix == 0, lambda step=step: hand_over(0, step))
             guarded(ix == n_x - 1, lambda step=step: hand_over(1, step))
+        if step == 1:
+            hand_on_corners()
     total = total + product(c_x - 2, 0)
     apply(c_x - 1, 1)
     own_ref[0, 0] = total + product(c_x - 1, 1)
@@ -382,26 +435,29 @@
         def _():
             from_face(d, 1).wait_recv()
 
-    half = c_y // 2
-    for d in range(4):
-        guarded(diagonals[d][0], lambda d=d: from_corner(d).wait_recv())
+    for d in (0, 1):
+        guarded(onward(d), lambda d=d: from_corner(d).wait_recv())
+    at_across(lambda d, side: from_across(d, side).wait_recv())
     for d in (0, 1):
         guarded(faces[d][0], lambda d=d: from_face(d, 0).wait_recv())
     corner_ref[0, 0] = along_lanes([row_dot(vc[d], rc[d]) for d in range(4)])
-    products = [block_dot(vx.at[d], 0, rx.at[d], 0, half) for d in range(2)]
+    products = [block_dot(vx.at[d], 0, rx.at[d], 0, direct) for d in range(2)]
     face_ref[0, 0, :, 0 : 2 * rows] = along_lanes(products)
     for d in (2, 3):
-        guarded(faces[d][0], lambda d=d: from_face(d, 0).wait_recv())
+        guarded(faces[d][0], lambda d=d: from_face(d, 1).wait_recv())
     for d in (0, 1):
         guarded(faces[d][0], lambda d=d: rest_x(d))
-    products = [block_dot(vx.at[d], half, rx.at[d], half, half) for d in range(2)]
+    products = [block_dot(vx.at[d], direct, rx.at[d], direct, c_y - direct) for d in range(2)]
     face_ref[0, 0, :, 0 : 2 * rows] += along_lanes(products)
     products = [block_dot(vy.at[d], 0, ry.at[d], 0, c_x) for d in range(2)]
     face_ref[0, 0, :, 2 * rows : 4 * rows] = along_lanes(products)
 
     def sent(d):
         to_face(d, 0).wait_send()
-        if d < 2:
+        if d >= 2:
+            to_face(d, 1).wait_send()
+        else:
+            guarded(onward(d), lambda: to_corner(d).wait_send())
 
             @pl.when(origin_of(d))
             def _():
@@ -414,7 +470,7 @@
 
     for d in range(4):
         guarded(faces[d][0], lambda d=d: sent(d))
-        guarded(diagonals[d][0], lambda d=d: to_corner(d).wait_send())
+    at_across(lambda d, side: to_across(d, side).wait_send())
 
     @pl.when(is_relay)
     def _():
@@ -461,8 +517,7 @@
             vmem((c_x, rows * (c_y + 1) + 7, c_z), F32),
             vmem((c_x, c_y, rows, c_z), BF16),
             vmem((2, c_y, rows, c_z), BF16),
-            vmem((c_x, rows, c_z), BF16),
-            vmem((c_x, rows, c_z), BF16),
+            vmem((2, c_x, rows, c_z), BF16),
             vmem((c_x + 2, c_y + 2, rows, c_z), F32),
             vmem((2, c_y, rows, c_z), BF16),
             vmem((2, c_y, rows, c_z), BF16),
@@ -470,7 +525,7 @@
             vmem((2, c_y, rows, c_z), BF16),
             vmem((2, c_x, rows, c_z), BF16),
             vmem((4, rows, c_z), BF16),
-            vmem((2, c_y // 4, rows, c_z), BF16),
+            vmem((2, (c_y - c_y * SHARE // 32) // 2, rows, c_z), BF16),
             vmem((4, rows, c_z), BF16),
             vmem((8, c_z), jnp.int32),
             vmem((n_y, 8, c_z), jnp.int32),
@@ -480,6 +535,7 @@
             pltpu.SemaphoreType.DMA((n_y,)),
             pltpu.SemaphoreType.DMA((n_y,)),
             pltpu.SemaphoreType.DMA((2, 2, 2)),
+            pltpu.SemaphoreType.DMA((2, 2)),
         ],
         compiler_params=pltpu.CompilerParams(
             collective_id=0, has_side_effects=True, vmem_limit_bytes=55040 * 1024

time: 18.6 us -> 18.5 us (level)
  no operation moved by 1% of the time
where the time goes in v8:
time: 18.5 us; the launch traced here: 18.4 us
  Pallas kernels  17.1 us (92%)
  between operations  1.29 us (7%)
    pallas_call x1, Pallas kernels, on_device(): pl.pallas_call(functools.partial(kernel, n_x, n_y), out_shape=results[:3]...  16.4 us
    pallas_call x1, Pallas kernels, on_device(): pl.pallas_call(hand_on, out_shape=results, in_specs=[anywhere] * 4, out_s...  0.71 us

profile of v8, /device:TPU:25, one launch (start us, length us, event | category | flops | bytes accessed | tf_op | source)
XLA Modules:
  0.0 18.4 jit_solution(11532169844855678174)
XLA Ops:
  1.3 16.4 %coarse.1 = (f32[1,1,64,64]{3,2,1,0:T(8,128)S(1)}, f32[1,1,64,256]{3,2,1,0:T(8,128)S(1)}, f32[1,1,64,256]{3,2,1,0:T(8,128)S(1)}, s32[8,128]{1,0:T(8,128)S(1)}) custom-call(bf16[64,8,32,128]{3,2,1,0:T(8,128)(2,1)} %vec_ref.1, f32[8,32,128]{2,1,0:T(8,128)} %rs_ref.1, f32[8,32,128]{2,1,0:T(8,128)} %dg_ref.1, s32[1,1]{1,0:T(1,128)S(6)} %copy.8.cnt_ref), custom_call_target="tpu_custom_call" | custom-call | flops 600000000 | bytes 5000000 | tf_op jit(solution)/shard_map/coarse/pallas_call | solution.py:508
  17.6 0.7 %results.1 = (f32[1,1,64,64]{3,2,1,0:T(8,128)}, f32[1,1,64,256]{3,2,1,0:T(8,128)}, f32[1,1,64,256]{3,2,1,0:T(8,128)}, s32[1,1]{1,0:T(1,128)}) custom-call(f32[1,1,64,64]{3,2,1,0:T(8,128)S(1)} %get-tuple-element.8.own_in, f32[1,1,64,256]{3,2,1,0:T(8,128)S(1)} %get-tuple-element.9.face_in, f32[1,1,64,256]{3,2,1,0:T(8,128)S(1)} %get-tuple-element.10.corner_in, ...), custom_call_target="tpu_custom_call" | custom-call | tf_op jit(solution)/shard_map/results/pallas_call | solution.py:546

commit v9 on v8

--- a/solution.py
+++ b/solution.py
@@ -64,6 +64,9 @@
     crecv_sem,
     relay_sem,
     across_sem,
+    sum_out,
+    sum_in,
+    tell_sem,
 ):
     rows, c_x, c_y, c_z = vec_ref.shape
     direct = c_y * SHARE // 32
@@ -105,11 +108,19 @@
         def _(device=device):
             pl.semaphore_signal(barrier, inc=1, device_id=device, device_id_type=MESH)
 
-    for far in range(2, n_y):
-
-        @pl.when(iy >= far)
+    mid = n_y // 2
+    upper = iy >= mid
+    slot = lax.rem(iy, mid)
+    is_teller = iy == mid - 1
+    for far in range(2, mid):
+
+        @pl.when(slot >= far)
         def _(far=far):
             pl.semaphore_signal(barrier, inc=1, device_id=(ix, iy - far), device_id_type=MESH)
+
+    @pl.when(iy > mid)
+    def _():
+        pl.semaphore_signal(barrier, inc=1, device_id=(ix, mid - 1), device_id_type=MESH)
 
     is_origin = (ix == across_low) | (ix == across_high)
     is_relay = (ix == 0) | (ix == n_x - 1)
@@ -149,7 +160,8 @@
                 pl.semaphore_signal(barrier, inc=1, device_id=across(d, side), device_id_type=MESH)
 
         greeted = greeted + ((at_once(0) | at_once(1)) & there).astype(jnp.int32)
-    greeted = greeted + jnp.maximum(n_y - 2 - iy, 0)
+    greeted = greeted + jnp.maximum(mid - 2 - slot, 0)
+    greeted = greeted + jnp.where(is_teller, n_y - mid - 1, 0)
 
     def zero_layers(ref):
         def step(i, _):
@@ -328,6 +340,8 @@
         def _():
             to_face(d, 1).start()
 
+    for far in range(1, mid):
+        guarded(slot + far < mid, lambda far=far: to_peer(far).start())
     for d in (3, 2):
         guarded(faces[d][0], lambda d=d: to_face(d, 0).start())
     at_across(lambda d, side: to_across(d, side).start())
@@ -335,8 +349,6 @@
         guarded(faces[d][0], lambda d=d: send_x(d))
     for d in (3, 2):
         guarded(faces[d][0], lambda d=d: to_face(d, 1).start())
-    for far in range(1, n_y):
-        guarded(iy + far < n_y, lambda far=far: to_peer(far).start())
 
     for side, x in enumerate((0, c_x - 1)):
         smoothed(x, [sx[side, y] for y in range(c_y)])
@@ -390,6 +402,32 @@
         apply(x + 2, 0)
         return total
 
+    def to_upper(other):
+        return pltpu.make_async_remote_copy(
+            src_ref=sum_out,
+            dst_ref=sum_in,
+            send_sem=tell_sem.at[other - mid],
+            recv_sem=tell_sem.at[n_y - mid],
+            device_id=(ix, other),
+            device_id_type=MESH,
+        )
+
+    def add_counts():
+        off_ref[...] = jnp.zeros(off_ref.shape, jnp.int32)
+        for far in range(1, mid):
+
+            def earlier(far=far):
+                to_peer(far).wait_recv()
+                off_ref[...] += cr[far]
+
+            guarded(slot >= far, earlier)
+
+        @pl.when(is_teller)
+        def _():
+            sum_out[...] = off_ref[...] + count
+            for other in range(mid, n_y):
+                to_upper(other).start()
+
     def hand_on_corners():
         for d in (2, 3):
             guarded(faces[d][0], lambda d=d: from_face(d, 0).wait_recv())
@@ -407,6 +445,7 @@
             guarded(ix == 0, lambda step=step: hand_over(0, step))
             guarded(ix == n_x - 1, lambda step=step: hand_over(1, step))
         if step == 1:
+            add_counts()
             hand_on_corners()
     total = total + product(c_x - 2, 0)
     apply(c_x - 1, 1)
@@ -415,15 +454,6 @@
     for d in range(4):
         x, y = (0, c_x - 1)[d // 2], (0, c_y - 1)[d % 2]
         vc[d] = (-0.25 * zp[x + 1, y + 1]).astype(BF16)
-
-    off_ref[...] = jnp.zeros(off_ref.shape, jnp.int32)
-    for far in range(1, n_y):
-
-        def earlier(far=far):
-            to_peer(far).wait_recv()
-            off_ref[...] += cr[far]
-
-        guarded(iy >= far, earlier)
 
     def rest_x(d):
         @pl.when(origin_of(d))
@@ -452,6 +482,11 @@
     products = [block_dot(vy.at[d], 0, ry.at[d], 0, c_x) for d in range(2)]
     face_ref[0, 0, :, 2 * rows : 4 * rows] = along_lanes(products)
 
+    @pl.when(upper)
+    def _():
+        to_upper(mid).wait_recv()
+        off_ref[...] += sum_in[...]
+
     def sent(d):
         to_face(d, 0).wait_send()
         if d >= 2:
@@ -477,8 +512,13 @@
         for chunk in range(2):
             by_relay(0, 1, chunk).wait_send()
 
-    for far in range(1, n_y):
-        guarded(iy + far < n_y, lambda far=far: to_peer(far).wait_send())
+    for far in range(1, mid):
+        guarded(slot + far < mid, lambda far=far: to_peer(far).wait_send())
+
+    @pl.when(is_teller)
+    def _():
+        for other in range(mid, n_y):
+            to_upper(other).wait_send()
 
 
 def hand_on(own_in, face_in, corner_in, off_in, own_out, face_out, corner_out, off_out, wide, first, sems):
@@ -536,6 +576,9 @@
             pltpu.SemaphoreType.DMA((n_y,)),
             pltpu.SemaphoreType.DMA((2, 2, 2)),
             pltpu.SemaphoreType.DMA((2, 2)),
+            vmem((8, c_z), jnp.int32),
+            vmem((8, c_z), jnp.int32),
+            pltpu.SemaphoreType.DMA((n_y - n_y // 2 + 1,)),
         ],
         compiler_params=pltpu.CompilerParams(
             collective_id=0, has_side_effects=True, vmem_limit_bytes=55040 * 1024

time: 18.5 us -> 17.7 us (0.957)
  the two profiles are of different devices: /device:TPU:25 before, /device:TPU:29 now
where the time goes in v9:
time: 17.7 us; the launch traced here: 17.6 us
  Pallas kernels  16.3 us (92%)
  between operations  1.29 us (7%)
    pallas_call x1, Pallas kernels, on_device(): pl.pallas_call(functools.partial(kernel, n_x, n_y), out_shape=results[:3]...  15.6 us
    pallas_call x1, Pallas kernels, on_device(): pl.pallas_call(hand_on, out_shape=results, in_specs=[anywhere] * 4, out_s...  0.71 us

profile of v9, /device:TPU:29, one launch (start us, length us, event | category | flops | bytes accessed | tf_op | source)
XLA Modules:
  0.0 17.6 jit_solution(16153094836173770308)
XLA Ops:
  1.3 15.6 %coarse.1 = (f32[1,1,64,64]{3,2,1,0:T(8,128)S(1)}, f32[1,1,64,256]{3,2,1,0:T(8,128)S(1)}, f32[1,1,64,256]{3,2,1,0:T(8,128)S(1)}, s32[8,128]{1,0:T(8,128)S(1)}) custom-call(bf16[64,8,32,128]{3,2,1,0:T(8,128)(2,1)} %vec_ref.1, f32[8,32,128]{2,1,0:T(8,128)} %rs_ref.1, f32[8,32,128]{2,1,0:T(8,128)} %dg_ref.1, s32[1,1]{1,0:T(1,128)S(6)} %copy.8.cnt_ref), custom_call_target="tpu_custom_call" | custom-call | flops 600000000 | bytes 5000000 | tf_op jit(solution)/shard_map/coarse/pallas_call | solution.py:548
  16.9 0.7 %results.1 = (f32[1,1,64,64]{3,2,1,0:T(8,128)}, f32[1,1,64,256]{3,2,1,0:T(8,128)}, f32[1,1,64,256]{3,2,1,0:T(8,128)}, s32[1,1]{1,0:T(1,128)}) custom-call(f32[1,1,64,64]{3,2,1,0:T(8,128)S(1)} %get-tuple-element.8.own_in, f32[1,1,64,256]{3,2,1,0:T(8,128)S(1)} %get-tuple-element.9.face_in, f32[1,1,64,256]{3,2,1,0:T(8,128)S(1)} %get-tuple-element.10.corner_in, ...), custom_call_target="tpu_custom_call" | custom-call | tf_op jit(solution)/shard_map/results/pallas_call | solution.py:589

commit v10 on v9

--- a/solution.py
+++ b/solution.py
@@ -440,10 +440,10 @@
 
     total = jnp.zeros((rows, rows), F32)
     for step in range(c_x // 2 - 1):
-        total = lax.fori_loop(step, step + 1, own_step, total)
         if step < 2:
             guarded(ix == 0, lambda step=step: hand_over(0, step))
             guarded(ix == n_x - 1, lambda step=step: hand_over(1, step))
+        total = lax.fori_loop(step, step + 1, own_step, total)
         if step == 1:
             add_counts()
             hand_on_corners()

time: 17.7 us -> 18 us (1.017)
  the two profiles are of different devices: /device:TPU:29 before, /device:TPU:1 now
where the time goes in v10:
time: 18 us; the launch traced here: 17.8 us
  Pallas kernels  16.6 us (92%)
  between operations  1.29 us (7%)
    pallas_call x1, Pallas kernels, on_device(): pl.pallas_call(functools.partial(kernel, n_x, n_y), out_shape=results[:3]...  15.8 us
    pallas_call x1, Pallas kernels, on_device(): pl.pallas_call(hand_on, out_shape=results, in_specs=[anywhere] * 4, out_s...  0.71 us

profile of v10, /device:TPU:1, one launch (start us, length us, event | category | flops | bytes accessed | tf_op | source)
XLA Modules:
  0.0 17.8 jit_solution(4361815357456474533)
XLA Ops:
  1.3 15.8 %coarse.1 = (f32[1,1,64,64]{3,2,1,0:T(8,128)S(1)}, f32[1,1,64,256]{3,2,1,0:T(8,128)S(1)}, f32[1,1,64,256]{3,2,1,0:T(8,128)S(1)}, s32[8,128]{1,0:T(8,128)S(1)}) custom-call(bf16[64,8,32,128]{3,2,1,0:T(8,128)(2,1)} %vec_ref.1, f32[8,32,128]{2,1,0:T(8,128)} %rs_ref.1, f32[8,32,128]{2,1,0:T(8,128)} %dg_ref.1, s32[1,1]{1,0:T(1,128)S(6)} %copy.8.cnt_ref), custom_call_target="tpu_custom_call" | custom-call | flops 600000000 | bytes 5000000 | tf_op jit(solution)/shard_map/coarse/pallas_call | solution.py:548
  17.1 0.7 %results.1 = (f32[1,1,64,64]{3,2,1,0:T(8,128)}, f32[1,1,64,256]{3,2,1,0:T(8,128)}, f32[1,1,64,256]{3,2,1,0:T(8,128)}, s32[1,1]{1,0:T(1,128)}) custom-call(f32[1,1,64,64]{3,2,1,0:T(8,128)S(1)} %get-tuple-element.8.own_in, f32[1,1,64,256]{3,2,1,0:T(8,128)S(1)} %get-tuple-element.9.face_in, f32[1,1,64,256]{3,2,1,0:T(8,128)S(1)} %get-tuple-element.10.corner_in, ...), custom_call_target="tpu_custom_call" | custom-call | tf_op jit(solution)/shard_map/results/pallas_call | solution.py:589
